TPU v7x, 128 devices: a whole 4x4x4 slice. The times are simulated.
128 devices in a mesh: rows: 16 (over x_hi, y, core), ctx: 8 (over x_lo, z).
Axes of the slice: x: 4 (x_hi: 2, x_lo: 2; x = x_hi * 2 + x_lo), y: 4, z: 4, core: 2. Of those that a mesh axis runs over, the one named last changes fastest.
Arguments:
- tokens: bfloat16 [2, 16, 1024, 1024], P(None, 'rows', 'ctx'), may hold values from -6 to 6
- cotangent: bfloat16 [2, 16, 1024, 1024], P(None, 'rows', 'ctx'), may hold values from -6 to 6
- bounds: int32 [2, 16, 5], P(None, 'rows'), may hold values from 0 to 1024, as said below
- positions: int32 [2, 16, 1024], P(None, 'rows', 'ctx'), may hold values from 0 to 1023, as said below
- norm_gain_attn: float32 [1024], replicated, may hold values from 0.5 to 1.5
- w_qkv: bfloat16 [1024, 2048], replicated, may hold values from -0.1875 to 0.1875
- qk_gain: float32 [128], replicated, may hold values from 0.5 to 1.5
- w_out: bfloat16 [1024, 1024], replicated, may hold values from -0.75 to 0.75
- norm_gain_ffn: float32 [1024], replicated, may hold values from 0.5 to 1.5
- w_gate_up: bfloat16 [1024, 9216], replicated, may hold values from -0.1875 to 0.1875
- w_down: bfloat16 [4608, 1024], replicated, may hold values from -0.09375 to 0.09375
Outputs:
- layer_out: bfloat16 [2, 16, 1024, 1024], P(None, 'rows', 'ctx')
- grad_tokens: float32 [2, 16, 1024, 1024], P(None, 'rows', 'ctx')
- grad_norm_attn: float32 [1024], P(('rows', 'ctx'))
- grad_qkv: float32 [1024, 2048], P(('rows', 'ctx'))
- grad_qk_gain: float32 [128], P(('rows', 'ctx'))
- grad_out: float32 [1024, 1024], P(('rows', 'ctx'))
- grad_norm_ffn: float32 [1024], P(('rows', 'ctx'))
- grad_gate_up: float32 [1024, 9216], P(('rows', 'ctx'))
- grad_down: float32 [4608, 1024], P(('rows', 'ctx'))
Inputs may be any that keep to these rules, and one draw needn't show every extreme that they name: `bounds`: in each row the offsets rise strictly; the first is 0 and the last is 1024; document k holds the tokens from offset k up to offset k + 1. `positions`: within a document the position rises by one from token to token.
All inputs are finite; a program needn't handle non-finite values.
Results may differ from a plain program's by a relative error of at most 0.035.
Values may be sent and summed in bfloat16 or wider, within the bound.
A program may use at most 256 MiB of HBM per device.

v0:
```python
import jax
import jax.numpy as jnp
from jax import lax
from jax.sharding import PartitionSpec as P

norm_eps = 1e-05
rope_theta = 1000000.0
masked_score = -1e30


def rms_scale(values):
    return lax.rsqrt(jnp.mean(values * values, axis=-1, keepdims=True) + norm_eps)


def rms_back(grad_normed, values, scale):
    normed = values * scale
    return scale * (grad_normed - normed * jnp.mean(grad_normed * normed, axis=-1, keepdims=True))


def rotary_tables(positions, width):
    half = width // 2
    freqs = rope_theta ** (-2.0 * jnp.arange(half, dtype=jnp.float32) / width)
    angles = positions.astype(jnp.float32)[:, None] * freqs[None, :]
    cosine = jnp.cos(angles)
    sine = jnp.sin(angles)
    return (jnp.concatenate([cosine, cosine], -1), jnp.concatenate([sine, sine], -1))


def rotate(values, cosine, sine):
    half = values.shape[-1] // 2
    turned = jnp.concatenate([-values[..., half:], values[..., :half]], -1)
    return values * cosine[:, None, :] + turned * sine[:, None, :]


def rotate_back(grads, cosine, sine):
    half = grads.shape[-1] // 2
    scaled = grads * sine[:, None, :]
    turned = jnp.concatenate([scaled[..., half:], -scaled[..., :half]], -1)
    return grads * cosine[:, None, :] + turned


def document_of(index, bounds_row):
    cuts = bounds_row[1:-1]
    return jnp.sum((index[:, None] >= cuts[None, :]).astype(jnp.int32), axis=1)


def contract_rows(left, right):
    return lax.dot_general(
        left, right, (((0,), (0,)), ((), ())), preferred_element_type=jnp.float32
    )


def contract_cols(left, right):
    return lax.dot_general(
        left, right, (((1,), (1,)), ((), ())), preferred_element_type=jnp.float32
    )


def local(
    tokens,
    cotangent,
    bounds,
    positions,
    norm_gain_attn,
    w_qkv,
    qk_gain,
    w_out,
    norm_gain_ffn,
    w_gate_up,
    w_down,
):
    micro = tokens.shape[0]
    rows_dev = tokens.shape[2]
    width = tokens.shape[3]
    cycle = lax.axis_size("ctx")
    seq = rows_dev * cycle
    head_dim = qk_gain.shape[0] // 2
    heads = w_out.shape[0] // head_dim
    kv_heads = (w_qkv.shape[1] - heads * head_dim) // (2 * head_dim)
    group = heads // kv_heads
    hidden_units = w_down.shape[0]
    q_width = heads * head_dim
    k_width = kv_heads * head_dim
    scale = head_dim ** (-0.5)
    block = 512
    blocks = seq // block
    all_rows = micro * rows_dev
    query_index = lax.axis_index("ctx") * rows_dev + jnp.arange(rows_dev, dtype=jnp.int32)
    key_index = jnp.arange(seq, dtype=jnp.int32)
    index_blocks = key_index.reshape(blocks, block)
    gain_query = qk_gain[:head_dim]
    gain_key = qk_gain[head_dim:]
    inputs = tokens[:, 0].reshape(all_rows, width).astype(jnp.float32)
    cosine, sine = rotary_tables(positions[:, 0].reshape(all_rows), head_dim)
    scale_attn = rms_scale(inputs)
    normed_attn = (inputs * scale_attn * norm_gain_attn).astype(jnp.bfloat16)
    projected = jnp.dot(normed_attn, w_qkv, preferred_element_type=jnp.float32)
    proj_query = projected[:, :q_width].reshape(all_rows, heads, head_dim)
    proj_key = projected[:, q_width : q_width + k_width].reshape(all_rows, kv_heads, head_dim)
    proj_value = projected[:, q_width + k_width :]
    scale_query = rms_scale(proj_query)
    scale_key = rms_scale(proj_key)
    queries = rotate(proj_query * scale_query * gain_query, cosine, sine).astype(jnp.bfloat16)
    keys_local = (
        rotate(proj_key * scale_key * gain_key, cosine, sine)
        .astype(jnp.bfloat16)
        .reshape(all_rows, k_width)
    )
    values_local = proj_value.astype(jnp.bfloat16)

    def masked_scores(query_four, query_doc, key_block, index_block, doc_block):
        scores = (
            jnp.einsum("kgqd,nkd->kgqn", query_four, key_block, preferred_element_type=jnp.float32)
            * scale
        )
        keep = (index_block[None, :] <= query_index[:, None]) & (
            doc_block[None, :] == query_doc[:, None]
        )
        return (jnp.where(keep, scores, masked_score), keep)

    query_fours = []
    query_docs = []
    doc_tables = []
    log_totals = []
    out_fours = []
    kept_pairs = []
    for step in range(micro):
        lower = step * rows_dev
        bounds_row = bounds[step, 0]
        query_doc = document_of(query_index, bounds_row)
        doc_blocks = document_of(key_index, bounds_row).reshape(blocks, block)
        query_four = (
            queries[lower : lower + rows_dev]
            .reshape(rows_dev, kv_heads, group, head_dim)
            .transpose(1, 2, 0, 3)
        )
        keys_all, values_all = (
            lax.all_gather(keys_local[lower : lower + rows_dev], "ctx", axis=0, tiled=True),
            lax.all_gather(values_local[lower : lower + rows_dev], "ctx", axis=0, tiled=True),
        )
        key_blocks = keys_all.reshape(blocks, block, kv_heads, head_dim)
        value_blocks = values_all.reshape(blocks, block, kv_heads, head_dim)

        def stats_step(carry, pieces):
            top, total = carry
            scores, keep = masked_scores(query_four, query_doc, pieces[0], pieces[1], pieces[2])
            new_top = jnp.maximum(top, jnp.max(scores, axis=-1))
            weights = jnp.where(keep, jnp.exp(scores - new_top[..., None]), 0.0)
            total = total * jnp.exp(top - new_top) + jnp.sum(weights, axis=-1)
            return ((new_top, total), None)

        start_top = jnp.full((kv_heads, group, rows_dev), masked_score, jnp.float32)
        start_total = jnp.zeros((kv_heads, group, rows_dev), jnp.float32)
        (top, total), unused = lax.scan(
            stats_step, (start_top, start_total), (key_blocks, index_blocks, doc_blocks)
        )
        log_total = top + jnp.log(total)

        def output_step(carry, pieces):
            scores, keep = masked_scores(query_four, query_doc, pieces[0], pieces[1], pieces[2])
            probs = jnp.where(keep, jnp.exp(scores - log_total[..., None]), 0.0).astype(
                jnp.bfloat16
            )
            carry = carry + jnp.einsum(
                "kgqn,nkd->kgqd", probs, pieces[3], preferred_element_type=jnp.float32
            )
            return (carry, None)

        start_out = jnp.zeros((kv_heads, group, rows_dev, head_dim), jnp.float32)
        out_four, unused = lax.scan(
            output_step, start_out, (key_blocks, index_blocks, doc_blocks, value_blocks)
        )
        query_fours.append(query_four)
        query_docs.append(query_doc)
        doc_tables.append(doc_blocks)
        log_totals.append(log_total)
        out_fours.append(out_four)
        kept_pairs.append((keys_all, values_all))
    attended_low = jnp.concatenate(
        [piece.transpose(2, 0, 1, 3).reshape(rows_dev, q_width) for piece in out_fours], 0
    ).astype(jnp.bfloat16)
    mid = inputs + jnp.dot(attended_low, w_out, preferred_element_type=jnp.float32)
    scale_ffn = rms_scale(mid)
    normed_ffn = (mid * scale_ffn * norm_gain_ffn).astype(jnp.bfloat16)
    gate_up = jnp.dot(normed_ffn, w_gate_up, preferred_element_type=jnp.float32)
    gate = gate_up[:, :hidden_units]
    upward = gate_up[:, hidden_units:]
    sigma = jax.nn.sigmoid(gate)
    hidden = (gate * sigma * upward).astype(jnp.bfloat16)
    layer_out = mid + jnp.dot(hidden, w_down, preferred_element_type=jnp.float32)
    grad_layer = cotangent[:, 0].reshape(all_rows, width).astype(jnp.float32)
    grad_low = grad_layer.astype(jnp.bfloat16)
    grad_down = contract_rows(hidden, grad_low)
    grad_hidden = contract_cols(grad_low, w_down)
    grad_gate = grad_hidden * upward * sigma * (1.0 + gate * (1.0 - sigma))
    grad_upward = grad_hidden * gate * sigma
    grad_gu_low = jnp.concatenate([grad_gate, grad_upward], -1).astype(jnp.bfloat16)
    grad_gate_up = contract_rows(normed_ffn, grad_gu_low)
    grad_nffn = contract_cols(grad_gu_low, w_gate_up)
    grad_gain_ffn = jnp.sum(grad_nffn * mid * scale_ffn, axis=0)
    grad_mid = grad_layer + rms_back(grad_nffn * norm_gain_ffn, mid, scale_ffn)
    grad_mid_low = grad_mid.astype(jnp.bfloat16)
    grad_out = contract_rows(attended_low, grad_mid_low)
    grad_attended = contract_cols(grad_mid_low, w_out).astype(jnp.bfloat16)
    query_grads = []
    key_grads = []
    value_grads = []
    for step in range(micro):
        lower = step * rows_dev
        query_four = query_fours[step]
        query_doc = query_docs[step]
        doc_blocks = doc_tables[step]
        log_total = log_totals[step]
        grad_four = (
            grad_attended[lower : lower + rows_dev]
            .reshape(rows_dev, kv_heads, group, head_dim)
            .transpose(1, 2, 0, 3)
        )
        delta = jnp.sum(grad_four.astype(jnp.float32) * out_fours[step], axis=-1)
        back_keys, back_values = (
            lax.all_gather(keys_local[lower : lower + rows_dev], "ctx", axis=0, tiled=True),
            lax.all_gather(values_local[lower : lower + rows_dev], "ctx", axis=0, tiled=True),
        )
        back_key_blocks = back_keys.reshape(blocks, block, kv_heads, head_dim)
        back_value_blocks = back_values.reshape(blocks, block, kv_heads, head_dim)

        def grad_step(carry, pieces):
            key_block, index_block, doc_block, value_block = pieces
            scores, keep = masked_scores(query_four, query_doc, key_block, index_block, doc_block)
            probs = jnp.where(keep, jnp.exp(scores - log_total[..., None]), 0.0)
            probs_low = probs.astype(jnp.bfloat16)
            grad_probs = jnp.einsum(
                "kgqd,nkd->kgqn", grad_four, value_block, preferred_element_type=jnp.float32
            )
            grad_scores = (probs * (grad_probs - delta[..., None])).astype(jnp.bfloat16)
            carry = (
                carry
                + jnp.einsum(
                    "kgqn,nkd->kgqd", grad_scores, key_block, preferred_element_type=jnp.float32
                )
                * scale
            )
            grad_key_block = (
                jnp.einsum(
                    "kgqn,kgqd->nkd", grad_scores, query_four, preferred_element_type=jnp.float32
                )
                * scale
            )
            grad_value_block = jnp.einsum(
                "kgqn,kgqd->nkd", probs_low, grad_four, preferred_element_type=jnp.float32
            )
            return (carry, (grad_key_block, grad_value_block))

        start_grad = jnp.zeros((kv_heads, group, rows_dev, head_dim), jnp.float32)
        grad_query_four, (grad_key_blocks, grad_value_blocks) = lax.scan(
            grad_step, start_grad, (back_key_blocks, index_blocks, doc_blocks, back_value_blocks)
        )
        grad_keys, grad_values = (
            lax.psum_scatter(
                grad_key_blocks.reshape(seq, k_width).astype(jnp.bfloat16),
                "ctx",
                scatter_dimension=0,
                tiled=True,
            ).astype(jnp.float32),
            lax.psum_scatter(
                grad_value_blocks.reshape(seq, k_width).astype(jnp.bfloat16),
                "ctx",
                scatter_dimension=0,
                tiled=True,
            ).astype(jnp.float32),
        )
        query_grads.append(grad_query_four.transpose(2, 0, 1, 3).reshape(rows_dev, heads, head_dim))
        key_grads.append(grad_keys)
        value_grads.append(grad_values)
    grad_query = jnp.concatenate(query_grads, 0)
    grad_keys = jnp.concatenate(key_grads, 0).reshape(all_rows, kv_heads, head_dim)
    grad_values = jnp.concatenate(value_grads, 0)
    grad_turn_query = rotate_back(grad_query, cosine, sine)
    grad_turn_key = rotate_back(grad_keys, cosine, sine)
    grad_gain_query = jnp.sum(grad_turn_query * proj_query * scale_query, axis=(0, 1))
    grad_gain_key = jnp.sum(grad_turn_key * proj_key * scale_key, axis=(0, 1))
    grad_proj_query = rms_back(grad_turn_query * gain_query, proj_query, scale_query).reshape(
        all_rows, q_width
    )
    grad_proj_key = rms_back(grad_turn_key * gain_key, proj_key, scale_key).reshape(
        all_rows, k_width
    )
    grad_projected = jnp.concatenate([grad_proj_query, grad_proj_key, grad_values], -1).astype(
        jnp.bfloat16
    )
    grad_qkv = contract_rows(normed_attn, grad_projected)
    grad_nattn = contract_cols(grad_projected, w_qkv)
    grad_gain_attn = jnp.sum(grad_nattn * inputs * scale_attn, axis=0)
    grad_inputs = grad_mid + rms_back(grad_nattn * norm_gain_attn, inputs, scale_attn)
    grad_qk = jnp.concatenate([grad_gain_query, grad_gain_key], 0)
    results = (
        lax.psum_scatter(grad_gain_attn, ("rows", "ctx"), scatter_dimension=0, tiled=True),
        lax.psum_scatter(grad_qkv, ("rows", "ctx"), scatter_dimension=0, tiled=True),
        lax.psum_scatter(grad_qk, ("rows", "ctx"), scatter_dimension=0, tiled=True),
        lax.psum_scatter(grad_out, ("rows", "ctx"), scatter_dimension=0, tiled=True),
        lax.psum_scatter(grad_gain_ffn, ("rows", "ctx"), scatter_dimension=0, tiled=True),
        lax.psum_scatter(grad_gate_up, ("rows", "ctx"), scatter_dimension=0, tiled=True),
        lax.psum_scatter(grad_down, ("rows", "ctx"), scatter_dimension=0, tiled=True),
    )
    layer_shard = layer_out.astype(jnp.bfloat16).reshape(micro, 1, rows_dev, width)
    input_shard = grad_inputs.reshape(micro, 1, rows_dev, width)
    return (
        layer_shard,
        input_shard,
        results[0],
        results[1],
        results[2],
        results[3],
        results[4],
        results[5],
        results[6],
    )


def solution(mesh):
    placed = (
        P(None, "rows", "ctx", None),
        P(None, "rows", "ctx", None),
        P(None, "rows", None),
        P(None, "rows", "ctx"),
        P(),
        P(),
        P(),
        P(),
        P(),
        P(),
        P(),
    )
    return jax.shard_map(
        local,
        mesh=mesh,
        in_specs=placed,
        out_specs=(
            P(None, "rows", "ctx", None),
            P(None, "rows", "ctx", None),
            P(("rows", "ctx")),
            P(("rows", "ctx"), None),
            P(("rows", "ctx")),
            P(("rows", "ctx"), None),
            P(("rows", "ctx")),
            P(("rows", "ctx"), None),
            P(("rows", "ctx"), None),
        ),
        check_vma=False,
    )
```

profile of v0, /device:TPU:1, one launch (start us, length us, event | category | flops | bytes accessed | tf_op | source)
XLA Modules:
  0.0 2469.4 jit_solution(4175771237719873441)
XLA Ops:
  11.4 4.6 fusion.153
  28.7 27.4 %all-gather.9.cloned.1.call-done = bf16[1024,512]{0,1:T(8,128)(2,1)} async-done(((bf16[128,512]{0,1:T(8,128)(2,1)}), bf16[1024,512]{0,1:T(8,128)(2,1)}) %all-gather.9.cloned.1.call-update) | async-done | bytes 1048592 | tf_op jit(solution)/shard_map/all_gather | solution.py:138
  59.2 38.0 %all-gather.5.cloned.1.call-done = bf16[1024,512]{0,1:T(8,128)(2,1)} async-done(((bf16[128,512]{0,1:T(8,128)(2,1)}), bf16[1024,512]{0,1:T(8,128)(2,1)}) %all-gather.5.cloned.1.call-update) | async-done | bytes 1048592 | tf_op jit(solution)/shard_map/all_gather | solution.py:138
  101.3 37.5 %all-gather.11.cloned.1.call-done = bf16[1024,512]{1,0:T(8,128)(2,1)} async-done(((bf16[128,512]{1,0:T(8,128)(2,1)}), bf16[1024,512]{1,0:T(8,128)(2,1)}) %all-gather.11.cloned.1.call-update) | async-done | bytes 1048592 | tf_op jit(solution)/shard_map/all_gather | solution.py:139
  138.8 3.9 reshape.299
  146.0 32.6 %all-gather.7.cloned.1.call-done = bf16[1024,512]{1,0:T(8,128)(2,1)} async-done(((bf16[128,512]{1,0:T(8,128)(2,1)}), bf16[1024,512]{1,0:T(8,128)(2,1)}) %all-gather.7.cloned.1.call-update) | async-done | bytes 1048592 | tf_op jit(solution)/shard_map/all_gather | solution.py:139
  185.8 6.5 while.80
  192.3 7.8 while.81
  200.0 4.2 while.78
  204.3 7.3 while.79
  215.9 9.6 fusion.145
  225.5 13.3 multiply_convert_fusion.1
  238.9 12.0 multiply_reduce_fusion
  259.9 25.0 %while.83 = (s32[]{:T(128)}, f32[8,2,128,64]{2,3,1,0:T(8,128)}, bf16[2,512,8,64]{1,3,2,0:T(8,128)(2,1)}, bf16[2,512,8,64]{1,3,2,0:T(8,128)(2,1)}, s32[2,512]{1,0...) while((s32[]{:T(128)}, f32[8,2,128,64]{2,3,1,0:T(8,128)}, ...), condition=%wide.region_26.27_spmd.clone, body=%wide.region_25.26_spmd.clone.sunk | while | flops 684523648 | bytes 41654092 | solution.py:255
  290.8 11.1 while.82
  336.4 4.1 multiply_reduce_fusion.1
  340.5 27.7 %reduce-scatter.10.cloned.1.call-done = bf16[128,512]{1,0:T(8,128)(2,1)} async-done(((bf16[1024,512]{1,0:T(8,128)(2,1)}), bf16[128,512]{1,0:T(8,128)(2,1)}) %reduce-scatter.10.cloned.1.call-update) | async-done | bytes 131088 | tf_op jit(solution)/shard_map/reduce_scatter | solution.py:259
  371.9 37.3 %reduce-scatter.16.cloned.1.call-done = bf16[128,512]{1,0:T(8,128)(2,1)} async-done(((bf16[1024,512]{1,0:T(8,128)(2,1)}), bf16[128,512]{1,0:T(8,128)(2,1)}) %reduce-scatter.16.cloned.1.call-update) | async-done | bytes 131088 | tf_op jit(solution)/shard_map/reduce_scatter | solution.py:265
  409.1 40.4 %reduce-scatter.14.cloned.1.call-done = bf16[128,512]{1,0:T(8,128)(2,1)} async-done(((bf16[1024,512]{1,0:T(8,128)(2,1)}), bf16[128,512]{1,0:T(8,128)(2,1)}) %reduce-scatter.14.cloned.1.call-update) | async-done | bytes 131088 | tf_op jit(solution)/shard_map/reduce_scatter | solution.py:265
  449.6 5.8 fusion.137
  456.6 17.5 fusion.123
  475.1 9.5 fusion.154
  484.6 371.1 %fusion.12 = f32[40,1024]{1,0:T(8,128)S(1)} fusion(f32[4608,1024]{1,0:T(8,128)} %fusion.154), kind=kCustom, calls=%all-reduce-scatter | all-reduce-scatter fusion | flops 5242881 | bytes 19038208
  862.9 13.8 collective-permute-start.7
  880.1 6.1 collective-permute-start.5
  896.7 7.8 fusion.125
  905.6 22.0 concatenate.77
  929.9 5.6 fusion.130
  935.5 81.4 %all-reduce.5 = (f32[1024]{0:T(1024)S(1)}, f32[128]{0:T(128)S(1)}, f32[1024]{0:T(1024)S(1)}) all-reduce(f32[1024]{0:T(1024)S(1)} %get-tuple-element.887, f32[128]{0:T(128)} %pad_maximum_fusion.11, f32[1024]{0:T(1024)S(1)} %copy-done.52), channel_id=6, replica_groups=mesh['rows'=16,'ctx'=8] {'rows','ctx'}, use_global_device_ids=true, to_apply=%region_35.36.clone | all-reduce | flops 2176 | bytes 17408
  1022.0 76.1 %reduce-scatter.20.cloned.1.call-done = f32[8,1024]{1,0:T(8,128)} async-done(((f32[1024,1024]{1,0:T(8,128)}), f32[8,1024]{1,0:T(8,128)}) %reduce-scatter.20.cloned.1.call-update) | async-done | bytes 32784 | tf_op jit(solution)/shard_map/reduce_scatter | solution.py:300
  1098.1 649.0 %reduce-scatter.18.cloned.1.call-done = f32[8,2048]{1,0:T(8,128)} async-done(((f32[1024,2048]{1,0:T(8,128)}), f32[8,2048]{1,0:T(8,128)}) %reduce-scatter.18.cloned.1.call-update) | async-done | bytes 65552 | tf_op jit(solution)/shard_map/reduce_scatter | solution.py:298
  1747.0 715.6 %reduce-scatter.22.cloned.1.call-done = f32[8,9216]{1,0:T(8,128)} async-done(((f32[1024,9216]{1,0:T(8,128)}), f32[8,9216]{1,0:T(8,128)}) %reduce-scatter.22.cloned.1.call-update) | async-done | bytes 294928 | tf_op jit(solution)/shard_map/reduce_scatter | solution.py:302
  (375 shorter events, 183.6 us)
Async XLA Ops:
  7.2 206.7 %copy-start = (bf16[1024,1024]{1,0:T(8,128)(2,1)S(1)}, bf16[1024,1024]{1,0:T(8,128)(2,1)}, u32[]{:S(2)}) copy-start(bf16[1024,1024]{1,0:T(8,128)(2,1)} %param.30) | copy-start | bytes 6291460
  7.2 48.8 %all-gather.9.cloned.1.call-start = ((), (), s32[]{:S(2)}) async-start(), calls=%async_computation.9 | async-start | bytes 1179648 | tf_op jit(solution)/shard_map/all_gather | solution.py:138
  19.2 78.1 %all-gather.5.cloned.1.call-start = ((), (), s32[]{:S(2)}) async-start(), calls=%async_computation.7 | async-start | bytes 1179648 | tf_op jit(solution)/shard_map/all_gather | solution.py:138
  19.9 118.9 %all-gather.11.cloned.1.call-start = ((), (), s32[]{:S(2)}) async-start(), calls=%async_computation.10 | async-start | bytes 1179648 | tf_op jit(solution)/shard_map/all_gather | solution.py:139
  21.7 156.9 %all-gather.7.cloned.1.call-start = ((), (), s32[]{:S(2)}) async-start(), calls=%async_computation.8 | async-start | bytes 1179648 | tf_op jit(solution)/shard_map/all_gather | solution.py:139
  22.3 318.2 %reduce-scatter.12.cloned.1.call-start = ((), (), s32[]{:S(2)}) async-start(), calls=%async_computation.12 | async-start | bytes 1179648 | tf_op jit(solution)/shard_map/reduce_scatter | solution.py:259
  26.8 31.2 %copy-start.40 = (f32[256,16]{0,1:T(8,128)}, f32[256,16]{0,1:T(8,128)S(1)}, u32[]{:S(2)}) copy-start(f32[256,16]{0,1:T(8,128)S(1)} %add_rsqrt_fusion) | copy-start | bytes 49156
  215.9 35.0 %copy-start.10 = (f32[256,1024]{1,0:T(8,128)}, f32[256,1024]{1,0:T(8,128)S(1)}, u32[]{:S(2)}) copy-start(f32[256,1024]{1,0:T(8,128)S(1)} %get-tuple-element.1078) | copy-start | bytes 3145732
  289.6 78.6 %reduce-scatter.10.cloned.1.call-start = ((), (), s32[]{:S(2)}) async-start(), calls=%async_computation.11 | async-start | bytes 1179648 | tf_op jit(solution)/shard_map/reduce_scatter | solution.py:259
  307.6 101.5 %reduce-scatter.16.cloned.1.call-start = ((), (), s32[]{:S(2)}) async-start(), calls=%async_computation.14 | async-start | bytes 1179648 | tf_op jit(solution)/shard_map/reduce_scatter | solution.py:265
  312.6 137.0 %reduce-scatter.14.cloned.1.call-start = ((), (), s32[]{:S(2)}) async-start(), calls=%async_computation.13 | async-start | bytes 1179648 | tf_op jit(solution)/shard_map/reduce_scatter | solution.py:265
  317.5 780.5 %reduce-scatter.20.cloned.1.call-start = ((), (), s32[]{:S(2)}) async-start(), calls=%async_computation.16 | async-start | bytes 4227072 | tf_op jit(solution)/shard_map/reduce_scatter | solution.py:300
  321.3 1425.7 %reduce-scatter.18.cloned.1.call-start = ((), (), s32[]{:S(2)}) async-start(), calls=%async_computation.15 | async-start | bytes 8454144 | tf_op jit(solution)/shard_map/reduce_scatter | solution.py:298
  336.4 33.1 %copy-start.15 = (f32[256,512]{0,1:T(8,128)S(1)}, f32[256,512]{0,1:T(8,128)}, u32[]{:S(2)}) copy-start(f32[256,512]{0,1:T(8,128)} %copy-done.14) | copy-start | bytes 1572868
  369.5 80.1 %copy-start.18 = (bf16[256,1024]{1,0:T(8,128)(2,1)S(1)}, bf16[256,1024]{1,0:T(8,128)(2,1)}, u32[]{:S(2)}) copy-start(bf16[256,1024]{1,0:T(8,128)(2,1)} %copy-done.17) | copy-start | bytes 1572868
  455.4 2007.3 %reduce-scatter.22.cloned.1.call-start = ((), (), s32[]{:S(2)}) async-start(), calls=%async_computation.17 | async-start | bytes 38043648 | tf_op jit(solution)/shard_map/reduce_scatter | solution.py:302
  855.7 21.0 collective-permute-start.11
  857.0 23.0 collective-permute-start.10
  858.4 4.6 collective-permute-start.12
  860.3 25.8 %collective-permute-start.9 = (f32[40,1024]{1,0:T(8,128)S(1)}, f32[40,1024]{1,0:T(8,128)S(1)}, u32[]{:S(2)}, u32[]{:S(2)}) collective-permute-start(f32[40,1024]{1,0:T(8,128)S(1)} %fusion.12), channel_id=1, source_target_pairs={{0,10},{1,11},{2,12},{3,13},{4,14},{5,15},{6,16},{7,17},{8,18},{9,... | collective-permute-start | bytes 491528
  861.6 26.5 %collective-permute-start.8 = (f32[40,1024]{1,0:T(8,128)S(1)}, f32[40,1024]{1,0:T(8,128)S(1)}, u32[]{:S(2)}, u32[]{:S(2)}) collective-permute-start(f32[40,1024]{1,0:T(8,128)S(1)} %fusion.12), channel_id=1, source_target_pairs={{0,9},{1,10},{2,11},{3,12},{4,13},{5,14},{6,15},{7,16},{8,17},{9,1... | collective-permute-start | bytes 491528
  862.9 27.1 %collective-permute-start.7 = (f32[40,1024]{1,0:T(8,128)S(1)}, f32[40,1024]{1,0:T(8,128)S(1)}, u32[]{:S(2)}, u32[]{:S(2)}) collective-permute-start(f32[40,1024]{1,0:T(8,128)S(1)} %fusion.12), channel_id=1, source_target_pairs={{0,8},{1,9},{2,10},{3,11},{4,12},{5,13},{6,14},{7,15},{8,16},{9,17... | collective-permute-start | bytes 491528
  876.7 15.2 collective-permute-start.6
  880.1 14.6 collective-permute-start.5
  886.1 18.4 collective-permute-start.4
  888.1 16.5 collective-permute-start.3
  890.0 14.6 collective-permute-start.2
  892.0 12.6 collective-permute-start.1
  894.7 10.9 collective-permute-start
  904.5 25.4 %copy-start.45 = (f32[1024]{0:T(1024)S(1)}, f32[1024]{0:T(1024)}, u32[]{:S(2)}) copy-start(f32[1024]{0:T(1024)} %param.27) | copy-start | bytes 12292
  904.5 25.4 %copy-start.51 = (f32[256]{0:T(256)S(1)}, f32[256]{0:T(256)}, u32[]{:S(2)}) copy-start(f32[256]{0:T(256)} %copy-done.50) | copy-start | bytes 3076
  929.9 1532.8 %copy-start.1 = (bf16[1024,1024]{1,0:T(8,128)(2,1)S(1)}, bf16[1024,1024]{1,0:T(8,128)(2,1)}, u32[]{:S(2)}) copy-start(bf16[1024,1024]{1,0:T(8,128)(2,1)} %param.30) | copy-start | bytes 6291460
  (57 other events, 263.7 us)
Sparse Core Ops, SparseCore 0:
  19.3 36.7 all-gather.8
  58.2 39.0 all-gather.4
  98.9 39.8 all-gather.10
  140.3 38.1 all-gather.6
  289.7 38.2 reduce-scatter.11
  330.2 37.9 reduce-scatter.9
  371.1 37.9 reduce-scatter.15
  411.5 37.9 reduce-scatter.13
  452.5 645.5 reduce-scatter.19
  1101.0 646.0 reduce-scatter.17
  1750.0 712.5 reduce-scatter.21
where the time goes:
time: 2490 us; the launch traced here: 2470 us
  waiting for transfers between devices  1680 us (67%)
  blocking collectives  453 us (18%)
  matrix products  143 us (6%)
  local copies, waits for them, and re-layouts  102 us (4%)
  starting transfers between devices  41.2 us (2%)
  other arithmetic  30.3 us (1%)
    reduce_scatter x1, waiting for transfers between devices, local(): lax.psum_scatter(grad_gate_up, ('rows', 'ctx'), scatter_dimension=0, tile...  716 us
    reduce_scatter x1, waiting for transfers between devices, local(): lax.psum_scatter(grad_qkv, ('rows', 'ctx'), scatter_dimension=0, tiled=True)  649 us
    unnamed x2, blocking collectives  453 us
    reduce_scatter x2, waiting for transfers between devices, local(): lax.psum_scatter(grad_value_blocks.reshape(seq, k_width).astype(jnp.bfloa...  77.7 us
    reduce_scatter x1, waiting for transfers between devices, local(): lax.psum_scatter(grad_out, ('rows', 'ctx'), scatter_dimension=0, tiled=True)  76.1 us
    all_gather x2, waiting for transfers between devices, local(): lax.all_gather(values_local[lower:lower + rows_dev], 'ctx', axis=0, tiled...  70.1 us
    all_gather x2, waiting for transfers between devices, local(): lax.all_gather(keys_local[lower:lower + rows_dev], 'ctx', axis=0, tiled=T...  65.4 us
  transfers between devices with their start and end apart: 24, of which 11 were waited for; matrix products, arithmetic and copies ran while one was open for 21% of the time, Pallas kernels for 0%

commit v1 on v0

--- a/solution.py
+++ b/solution.py
@@ -1,11 +1,677 @@
+import functools
+
 import jax
 import jax.numpy as jnp
 from jax import lax
+from jax.experimental import pallas as pl
+from jax.experimental.pallas import tpu as pltpu
 from jax.sharding import PartitionSpec as P
 
+MESH = pl.DeviceIdType.MESH
 norm_eps = 1e-05
 rope_theta = 1000000.0
 masked_score = -1e30
+f32 = jnp.float32
+bf16 = jnp.bfloat16
+VMEM_LIMIT = 64 * 2**20 - 2**18
+
+
+class Place:
+    def __init__(self):
+        r = lax.axis_index("rows")
+        k = lax.axis_index("ctx")
+        self.x_hi = lax.div(r, 8)
+        self.y = lax.rem(lax.div(r, 2), 4)
+        self.core = lax.rem(r, 2)
+        self.x_lo = lax.div(k, 4)
+        self.z = lax.rem(k, 4)
+        self.rows = r
+        self.ctx = k
+        self.bits = [
+            self.x_hi,
+            lax.rem(self.x_hi + self.x_lo, 2),
+            lax.div(self.y, 2),
+            lax.rem(lax.div(self.y, 2) + lax.rem(self.y, 2), 2),
+            lax.div(self.z, 2),
+            lax.rem(lax.div(self.z, 2) + lax.rem(self.z, 2), 2),
+        ]
+
+    def at(self, x_hi=None, x_lo=None, y=None, z=None, core=None):
+        x_hi = self.x_hi if x_hi is None else x_hi
+        x_lo = self.x_lo if x_lo is None else x_lo
+        y = self.y if y is None else y
+        z = self.z if z is None else z
+        core = self.core if core is None else core
+        return (x_hi * 8 + y * 2 + core, x_lo * 4 + z)
+
+    def partner(self):
+        return self.at(core=1 - self.core)
+
+    def neighbour(self, dim):
+        if dim == 0:
+            return self.at(x_hi=1 - self.x_hi, x_lo=1 - self.x_lo)
+        if dim == 1:
+            return self.at(x_lo=1 - self.x_lo)
+        if dim == 2:
+            return self.at(y=3 - self.y)
+        if dim == 3:
+            return self.at(y=self.y + 1 - 2 * lax.rem(self.y, 2))
+        if dim == 4:
+            return self.at(z=3 - self.z)
+        return self.at(z=self.z + 1 - 2 * lax.rem(self.z, 2))
+
+
+def gray(v):
+    return v ^ (v >> 1)
+
+
+def chip_number(x_hi, x_lo, y, z):
+    return gray(2 * x_hi + x_lo) * 16 + gray(y) * 4 + gray(z)
+
+
+def slot_of(number, s):
+    turned = number << s
+    return (turned & 63) | (turned >> 6)
+
+
+HELD_AT = [64 - (64 >> t) for t in range(7)]
+
+
+class Scatter:
+    def __init__(self, place, first, held, send_sems, recv_sems, per):
+        self.place = place
+        self.first = first
+        self.held = held
+        self.send_sems = send_sems
+        self.recv_sems = recv_sems
+        self.per = per
+
+    def part(self, s, t, which):
+        half = 32 >> t
+        if t == 0:
+            return self.first, which * half
+        return self.held, HELD_AT[t - 1] + which * half
+
+    def copy(self, s, t):
+        half = 32 >> t
+        dim = (s + t) % 6
+        ref, start = self.part(s, t, 1 - self.place.bits[dim])
+        return pltpu.make_async_remote_copy(
+            src_ref=ref.at[s, pl.ds(start, half)],
+            dst_ref=self.held.at[s, pl.ds(HELD_AT[t], half)],
+            send_sem=self.send_sems.at[s, t],
+            recv_sem=self.recv_sems.at[s, t],
+            device_id=self.place.neighbour(dim),
+            device_id_type=MESH,
+        )
+
+    def send(self, s, t):
+        self.copy(s, t).start()
+
+    def take(self, s, t):
+        self.copy(s, t).wait_recv()
+        half = 32 >> t
+        ref, start = self.part(s, t, self.place.bits[(s + t) % 6])
+        per = min(self.per, half)
+
+        def body(i, carry):
+            for j in range(per):
+                at = i * per + j
+                self.held[s, HELD_AT[t] + at] = (
+                    self.held[s, HELD_AT[t] + at].astype(f32) + ref[s, start + at].astype(f32)
+                ).astype(bf16)
+            return carry
+
+        lax.fori_loop(0, half // per, body, 0)
+        self.send(s, t + 1)
+
+    def last(self, s):
+        self.copy(s, 5).wait_recv()
+        ref, start = self.part(s, 5, self.place.bits[(s + 5) % 6])
+        return self.held[s, HELD_AT[5]].astype(f32) + ref[s, start].astype(f32)
+
+    def sent(self):
+        for s in range(6):
+            for t in range(6):
+                self.copy(s, t).wait_send()
+
+
+def greet(devices):
+    barrier = pltpu.get_barrier_semaphore()
+    for device in devices:
+        pl.semaphore_signal(barrier, inc=1, device_id=device, device_id_type=MESH)
+    pl.semaphore_wait(barrier, len(devices))
+
+
+def greet_all(place, devices):
+    barrier = pltpu.get_barrier_semaphore()
+    targets = down_targets(place)
+    for device in devices + targets[1:]:
+        pl.semaphore_signal(barrier, inc=1, device_id=device, device_id_type=MESH)
+    swapped = place.x_hi != place.core
+    count = len(devices) + 3
+
+    @pl.when(swapped)
+    def _():
+        pl.semaphore_signal(barrier, inc=1, device_id=targets[0], device_id_type=MESH)
+        pl.semaphore_wait(barrier, count + 1)
+
+    @pl.when(jnp.logical_not(swapped))
+    def _():
+        pl.semaphore_wait(barrier, count)
+
+
+def push(place, src, dst, send_sem, recv_sem, device):
+    return pltpu.make_async_remote_copy(
+        src_ref=src,
+        dst_ref=dst,
+        send_sem=send_sem,
+        recv_sem=recv_sem,
+        device_id=device,
+        device_id_type=MESH,
+    )
+
+
+def down_targets(place):
+    return [
+        place.at(x_hi=place.core, core=place.x_hi, z=lax.rem(place.z + off, 4)) for off in range(4)
+    ]
+
+
+def dot(left, right):
+    return jnp.dot(left, right, preferred_element_type=f32)
+
+
+def dot_cols(left, right):
+    return lax.dot_general(left, right, (((1,), (1,)), ((), ())), preferred_element_type=f32)
+
+
+FF_HALF = 2304
+
+
+def ffn_kernel(
+    mid_ref,
+    cot_ref,
+    gain_ref,
+    wgu_hbm,
+    wd_hbm,
+    out_ref,
+    dmid_ref,
+    ggain_ref,
+    ggu_ref,
+    gdn_ref,
+    wgu,
+    wd,
+    nf,
+    nft,
+    dyb,
+    h,
+    ht,
+    dgu,
+    sum_own,
+    sum_send,
+    sum_recv,
+    g_first,
+    g_held,
+    d_first,
+    d_held,
+    g_fin,
+    g_in,
+    d_acc,
+    d_stage,
+    d_in,
+    w_sems,
+    x_send,
+    x_recv,
+    g_send,
+    g_recv,
+    d_send,
+    d_recv,
+    f_send,
+    f_recv,
+):
+    place = Place()
+    core = place.core
+    loads = []
+    for i in range(3):
+        at = pl.multiple_of(core * FF_HALF + 768 * i, 256)
+        loads.append(
+            [
+                pltpu.make_async_copy(
+                    wgu_hbm.at[:, pl.ds(at, 768)], wgu.at[:, pl.ds(768 * i, 768)], w_sems.at[3 * i]
+                ),
+                pltpu.make_async_copy(
+                    wgu_hbm.at[:, pl.ds(pl.multiple_of(4608 + at, 256), 768)],
+                    wgu.at[:, pl.ds(FF_HALF + 768 * i, 768)],
+                    w_sems.at[3 * i + 1],
+                ),
+                pltpu.make_async_copy(
+                    wd_hbm.at[pl.ds(at, 768)], wd.at[pl.ds(768 * i, 768)], w_sems.at[3 * i + 2]
+                ),
+            ]
+        )
+        for copy in loads[-1]:
+            copy.start()
+
+    greet_all(place, [place.partner()] + [place.neighbour(dim) for dim in range(6)])
+
+    partner = place.partner()
+    to_dy = push(place, cot_ref, dyb.at[pl.ds(256, 256)], x_send.at[0], x_recv.at[0], partner)
+    to_dy.start()
+    mid = mid_ref[...]
+    scale = lax.rsqrt(jnp.mean(mid * mid, axis=-1, keepdims=True) + norm_eps)
+    nf[pl.ds(0, 256), :] = (mid * scale * gain_ref[...]).astype(bf16)
+    dyb[pl.ds(0, 256), :] = cot_ref[...]
+    to_nf = push(
+        place,
+        nf.at[pl.ds(0, 256)],
+        nf.at[pl.ds(256, 256)],
+        x_send.at[1],
+        x_recv.at[1],
+        partner,
+    )
+    to_nf.start()
+    to_dy.wait_recv()
+    to_nf.wait_recv()
+    for i in range(2):
+        nft[:, pl.ds(256 * i, 256)] = nf[pl.ds(256 * i, 256), :].T
+
+    for i in range(3):
+        for copy in loads[i]:
+            copy.wait()
+
+        def units(j, carry, i=i):
+            at = pl.multiple_of(768 * i + 256 * j, 256)
+            gate = dot(nf[...], wgu[:, pl.ds(at, 256)])
+            upward = dot(nf[...], wgu[:, pl.ds(pl.multiple_of(FF_HALF + at, 256), 256)])
+            grad_hidden = dot_cols(dyb[...], wd[pl.ds(at, 256), :])
+            sigma = 1.0 / (1.0 + jnp.exp(-gate))
+            silu = gate * sigma
+            hidden = (silu * upward).astype(bf16)
+            h[:, pl.ds(at, 256)] = hidden
+            ht[pl.ds(at, 256), :] = hidden.T
+            dgu[:, pl.ds(at, 256)] = (
+                grad_hidden * upward * (sigma + silu * (1.0 - sigma))
+            ).astype(bf16)
+            dgu[:, pl.ds(pl.multiple_of(FF_HALF + at, 256), 256)] = (grad_hidden * silu).astype(bf16)
+            return carry
+
+        lax.fori_loop(0, 3, units, 0)
+
+    down = Scatter(place, d_first, d_held, d_send, d_recv, 4)
+    for block in range(3):
+
+        def down_cols(z, carry, block=block):
+            part = dot(
+                ht[pl.ds(768 * block, 768), :], dyb[:, pl.ds(pl.multiple_of(256 * z, 256), 256)]
+            )
+            z_number = 2 * lax.div(z, 2) + lax.rem(lax.div(z, 2) + lax.rem(z, 2), 2)
+            for i in range(16):
+                q = 16 * block + i
+                y, core_to, x_lo, rg = q // 12, (q // 6) % 2, (q // 3) % 2, q % 3
+                number = chip_number(core_to, x_lo, y, 0) + z_number
+                for ch in range(2):
+                    s = 2 * rg + ch
+                    turned = number * (1 << s)
+                    slot = lax.rem(turned, 64) + lax.div(turned, 64)
+                    d_first[s, slot] = part[48 * i : 48 * i + 48, 128 * ch : 128 * ch + 128].astype(
+                        bf16
+                    )
+            return carry
+
+        lax.fori_loop(0, 4, down_cols, 0)
+    for s in range(6):
+        down.send(s, 0)
+
+    both = Scatter(place, g_first, g_held, g_send, g_recv, 2)
+    for s in range(6):
+
+        def gate_cols(j, carry, s=s):
+            cols = dgu[:, pl.ds(pl.multiple_of(768 * s + 256 * j, 256), 256)]
+            for x_hi in range(2):
+                part = dot(nft[pl.ds(512 * x_hi, 512), :], cols)
+                part = part.reshape(4, 2, 8, 8, 256)
+                for y in range(4):
+                    for x_lo in range(2):
+                        for z in range(4):
+                            slot = slot_of(chip_number(x_hi, x_lo, y, z), s)
+                            piece = part[y, :, 4 * x_lo + z].reshape(16, 256)
+                            g_first[s, slot, :, pl.ds(pl.multiple_of(256 * j, 256), 256)] = piece.astype(
+                                bf16
+                            )
+            return carry
+
+        lax.fori_loop(0, 3, gate_cols, 0)
+        both.send(s, 0)
+
+    def out_cols(j, carry):
+        at = pl.ds(pl.multiple_of(256 * j, 256), 256)
+        part = dot(h[...], wd[:, at])
+        sum_own[:, at] = part[:256]
+        sum_send[0, :, at] = part[256:].astype(bf16)
+        return carry
+
+    lax.fori_loop(0, 4, out_cols, 0)
+    to_out = push(place, sum_send.at[0], sum_recv.at[0], x_send.at[2], x_recv.at[2], partner)
+    to_out.start()
+
+    def back_cols(j, carry):
+        at = pl.ds(pl.multiple_of(256 * j, 256), 256)
+        part = dot_cols(dgu[...], wgu[at, :])
+        dmid_ref[:, at] = part[:256]
+        sum_send[1, :, at] = part[256:].astype(bf16)
+        return carry
+
+    lax.fori_loop(0, 4, back_cols, 0)
+    to_back = push(place, sum_send.at[1], sum_recv.at[1], x_send.at[3], x_recv.at[3], partner)
+    to_back.start()
+    to_out.wait_recv()
+    out_ref[...] = (mid_ref[...] + sum_own[...] + sum_recv[0].astype(f32)).astype(bf16)
+    to_back.wait_recv()
+    mid = mid_ref[...]
+    scale = lax.rsqrt(jnp.mean(mid * mid, axis=-1, keepdims=True) + norm_eps)
+    normed = mid * scale
+    grad_nffn = dmid_ref[...] + sum_recv[1].astype(f32)
+    ggain_ref[...] = jnp.sum(grad_nffn * normed, axis=0, keepdims=True)
+    grad_e = grad_nffn * gain_ref[...]
+    dmid_ref[...] = cot_ref[...].astype(f32) + scale * (
+        grad_e - normed * jnp.mean(grad_e * normed, axis=-1, keepdims=True)
+    )
+
+    for t in range(5):
+        for s in range(6):
+            down.take(s, t)
+        for s in range(6):
+            both.take(s, t)
+    finish_down(place, down, d_acc, d_stage, d_in, f_send, f_recv, gdn_ref)
+    for s in range(6):
+        total = both.last(s)
+        g_fin[0, s] = total[:8]
+        g_fin[1, s] = total[8:]
+    swap = push(place, g_fin.at[1 - core], g_in, x_send.at[4], x_recv.at[4], partner)
+    swap.start()
+    for s in range(6):
+        base = (s // 3) * 4608 + (s % 3) * 768
+        at = pl.multiple_of(base + core * FF_HALF, 256)
+        ggu_ref[:, pl.ds(at, 768)] = g_fin[core, s]
+    swap.wait_recv()
+    for s in range(6):
+        base = (s // 3) * 4608 + (s % 3) * 768
+        at = pl.multiple_of(base + (1 - core) * FF_HALF, 256)
+        ggu_ref[:, pl.ds(at, 768)] = g_in[s]
+    to_dy.wait_send()
+    to_nf.wait_send()
+    to_out.wait_send()
+    to_back.wait_send()
+    swap.wait_send()
+    down.sent()
+    both.sent()
+
+
+def finish_down(place, down, d_acc, d_stage, d_in, f_send, f_recv, gdn_ref):
+    for s in range(6):
+        d_acc[pl.ds(48 * (s // 2), 48), pl.ds(128 * (s % 2), 128)] = down.last(s)
+    for z in range(4):
+        d_stage[z, pl.ds(0, 36), :] = d_acc[pl.ds(36 * z, 36), :]
+        d_stage[z, pl.ds(36, 4), :] = jnp.zeros((4, 256), f32)
+    targets = down_targets(place)
+    swapped = place.x_hi != place.core
+    moves = []
+    for off in range(4):
+        moves.append(
+            push(
+                place,
+                d_stage.at[lax.rem(place.z + off, 4)],
+                d_in.at[place.z],
+                f_send.at[off],
+                f_recv.at[off],
+                targets[off],
+            )
+        )
+    for off in range(1, 4):
+        moves[off].start()
+
+    @pl.when(swapped)
+    def _():
+        moves[0].start()
+        moves[0].wait_recv()
+
+    @pl.when(jnp.logical_not(swapped))
+    def _():
+        d_in[place.z] = d_stage[place.z]
+
+    for off in range(1, 4):
+        moves[off].wait_recv()
+    for z in range(4):
+        gdn_ref[:, pl.ds(256 * z, 256)] = d_in[z, pl.ds(0, 36), :]
+    for off in range(1, 4):
+        moves[off].wait_send()
+
+    @pl.when(swapped)
+    def _():
+        moves[0].wait_send()
+
+
+def ffn(mid, cot, gain, w_gate_up, w_down):
+    vmem = pl.BlockSpec(memory_space=pltpu.VMEM)
+    hbm = pl.BlockSpec(memory_space=pl.ANY)
+    dma = pltpu.SemaphoreType.DMA
+    return pl.pallas_call(
+        ffn_kernel,
+        out_shape=(
+            jax.ShapeDtypeStruct((256, 1024), bf16),
+            jax.ShapeDtypeStruct((256, 1024), f32),
+            jax.ShapeDtypeStruct((1, 1024), f32),
+            jax.ShapeDtypeStruct((8, 9216), f32),
+            jax.ShapeDtypeStruct((36, 1024), f32),
+        ),
+        in_specs=[vmem, vmem, vmem, hbm, hbm],
+        out_specs=(vmem, vmem, vmem, vmem, vmem),
+        scratch_shapes=[
+            pltpu.VMEM((1024, 4608), bf16),
+            pltpu.VMEM((FF_HALF, 1024), bf16),
+            pltpu.VMEM((512, 1024), bf16),
+            pltpu.VMEM((1024, 512), bf16),
+            pltpu.VMEM((512, 1024), bf16),
+            pltpu.VMEM((512, FF_HALF), bf16),
+            pltpu.VMEM((FF_HALF, 512), bf16),
+            pltpu.VMEM((512, 4608), bf16),
+            pltpu.VMEM((256, 1024), f32),
+            pltpu.VMEM((2, 256, 1024), bf16),
+            pltpu.VMEM((2, 256, 1024), bf16),
+            pltpu.VMEM((6, 64, 16, 768), bf16),
+            pltpu.VMEM((6, 63, 16, 768), bf16),
+            pltpu.VMEM((6, 64, 48, 128), bf16),
+            pltpu.VMEM((6, 63, 48, 128), bf16),
+            pltpu.VMEM((2, 6, 8, 768), f32),
+            pltpu.VMEM((6, 8, 768), f32),
+            pltpu.VMEM((144, 256), f32),
+            pltpu.VMEM((4, 40, 256), f32),
+            pltpu.VMEM((4, 40, 256), f32),
+            dma((9,)),
+            dma((5,)),
+            dma((5,)),
+            dma((6, 6)),
+            dma((6, 6)),
+            dma((6, 6)),
+            dma((6, 6)),
+            dma((4,)),
+            dma((4,)),
+        ],
+        compiler_params=pltpu.CompilerParams(
+            collective_id=0, has_side_effects=True, vmem_limit_bytes=VMEM_LIMIT
+        ),
+        name="feed_forward",
+    )(mid, cot, gain, w_gate_up, w_down)
+
+
+def reorder_store(part, first, s, x_hi, at, width):
+    part = part.reshape(4, 2, 8, 8, width)
+    for y in range(4):
+        for x_lo in range(2):
+            for z in range(4):
+                slot = slot_of(chip_number(x_hi, x_lo, y, z), s)
+                first[s, slot, :, at] = part[y, :, 4 * x_lo + z].reshape(16, width).astype(bf16)
+
+
+def last_kernel(
+    x_ref,
+    dmid_ref,
+    na_ref,
+    dp_ref,
+    att_ref,
+    gain_ref,
+    vec_ref,
+    w_qkv,
+    gtok_ref,
+    gqkv_ref,
+    gout_ref,
+    vec_out,
+    xin,
+    dpin,
+    dmin,
+    dm_own,
+    nat,
+    attt,
+    cols,
+    q_first,
+    q_held,
+    q_fin,
+    q_in,
+    vec,
+    vec_in,
+    x_send,
+    x_recv,
+    q_send,
+    q_recv,
+    v_send,
+    v_recv,
+):
+    place = Place()
+    core = place.core
+    partner = place.partner()
+    greet([partner] + [place.neighbour(dim) for dim in range(6)])
+    for half in range(2):
+        dm_own[half] = dmid_ref[:, pl.ds(512 * half, 512)].astype(bf16)
+    moves = [
+        push(place, na_ref, xin.at[0], x_send.at[0], x_recv.at[0], partner),
+        push(place, att_ref, xin.at[1], x_send.at[1], x_recv.at[1], partner),
+        push(place, dp_ref.at[1 - core], dpin, x_send.at[2], x_recv.at[2], partner),
+        push(place, dm_own.at[1 - core], dmin, x_send.at[3], x_recv.at[3], partner),
+    ]
+    for move in moves:
+        move.start()
+    nat[:, pl.ds(0, 256)] = na_ref[...].T
+    attt[:, pl.ds(0, 256)] = att_ref[...].T
+    cols[pl.ds(0, 256), pl.ds(0, 1024)] = dp_ref[core]
+    cols[pl.ds(0, 256), pl.ds(1024, 512)] = dm_own[core]
+    for move in moves:
+        move.wait_recv()
+    nat[:, pl.ds(256, 256)] = xin[0].T
+    attt[:, pl.ds(256, 256)] = xin[1].T
+    cols[pl.ds(256, 256), pl.ds(0, 1024)] = dpin[...]
+    cols[pl.ds(256, 256), pl.ds(1024, 512)] = dmin[...]
+    quad = Scatter(place, q_first, q_held, q_send, q_recv, 4)
+    for s in range(6):
+        left = nat if s < 4 else attt
+        for x_hi in range(2):
+            part = dot(left[pl.ds(512 * x_hi, 512), :], cols[:, pl.ds(256 * s, 256)])
+            reorder_store(part, q_first, s, x_hi, slice(None), 256)
+        quad.send(s, 0)
+
+    inputs = x_ref[...].astype(f32)
+    scale = lax.rsqrt(jnp.mean(inputs * inputs, axis=-1, keepdims=True) + norm_eps)
+    normed = inputs * scale
+    grad_n = dot_cols(dp_ref[0], w_qkv[:, pl.ds(0, 1024)]) + dot_cols(
+        dp_ref[1], w_qkv[:, pl.ds(1024, 1024)]
+    )
+    gain_grad = jnp.sum(grad_n * normed, axis=0, keepdims=True)
+    grad_e = grad_n * gain_ref[...]
+    gtok_ref[...] = dmid_ref[...] + scale * (
+        grad_e - normed * jnp.mean(grad_e * normed, axis=-1, keepdims=True)
+    )
+    vec[0, pl.ds(8, 16), :] = vec_ref[pl.ds(8, 16), :]
+    for i in range(8):
+        vec[0, pl.ds(i, 1), :] = gain_grad[:, 128 * i : 128 * i + 128]
+
+    def vec_move(step):
+        device = place.neighbour(step) if step < 6 else partner
+        return push(place, vec.at[step], vec_in.at[step], v_send.at[step], v_recv.at[step], device)
+
+    vec_move(0).start()
+    for t in range(5):
+        for s in range(6):
+            quad.take(s, t)
+        vec_move(t).wait_recv()
+        vec[t + 1] = vec[t] + vec_in[t]
+        vec_move(t + 1).start()
+    for s in range(6):
+        total = quad.last(s)
+        q_fin[0, s] = total[:8]
+        q_fin[1, s] = total[8:]
+    swap = push(place, q_fin.at[1 - core], q_in, x_send.at[4], x_recv.at[4], partner)
+    swap.start()
+    vec_move(5).wait_recv()
+    vec[6] = vec[5] + vec_in[5]
+    vec_move(6).start()
+    for s in range(4):
+        gqkv_ref[:, pl.ds(pl.multiple_of(core * 1024 + 256 * s, 256), 256)] = q_fin[core, s]
+    for s in range(4, 6):
+        gout_ref[:, pl.ds(pl.multiple_of(core * 512 + 256 * (s - 4), 256), 256)] = q_fin[core, s]
+    swap.wait_recv()
+    for s in range(4):
+        gqkv_ref[:, pl.ds(pl.multiple_of((1 - core) * 1024 + 256 * s, 256), 256)] = q_in[s]
+    for s in range(4, 6):
+        gout_ref[:, pl.ds(pl.multiple_of((1 - core) * 512 + 256 * (s - 4), 256), 256)] = q_in[s]
+    vec_move(6).wait_recv()
+    vec_out[...] = vec[6] + vec_in[6]
+    for move in moves:
+        move.wait_send()
+    swap.wait_send()
+    for step in range(7):
+        vec_move(step).wait_send()
+    quad.sent()
+
+
+def last_part(x, dmid, na, dp, att, gain, vec, w_qkv):
+    vmem = pl.BlockSpec(memory_space=pltpu.VMEM)
+    dma = pltpu.SemaphoreType.DMA
+    return pl.pallas_call(
+        last_kernel,
+        out_shape=(
+            jax.ShapeDtypeStruct((256, 1024), f32),
+            jax.ShapeDtypeStruct((8, 2048), f32),
+            jax.ShapeDtypeStruct((8, 1024), f32),
+            jax.ShapeDtypeStruct((24, 128), f32),
+        ),
+        in_specs=[vmem] * 8,
+        out_specs=(vmem,) * 4,
+        scratch_shapes=[
+            pltpu.VMEM((2, 256, 1024), bf16),
+            pltpu.VMEM((256, 1024), bf16),
+            pltpu.VMEM((256, 512), bf16),
+            pltpu.VMEM((2, 256, 512), bf16),
+            pltpu.VMEM((1024, 512), bf16),
+            pltpu.VMEM((1024, 512), bf16),
+            pltpu.VMEM((512, 1536), bf16),
+            pltpu.VMEM((6, 64, 16, 256), bf16),
+            pltpu.VMEM((6, 63, 16, 256), bf16),
+            pltpu.VMEM((2, 6, 8, 256), f32),
+            pltpu.VMEM((6, 8, 256), f32),
+            pltpu.VMEM((7, 24, 128), f32),
+            pltpu.VMEM((7, 24, 128), f32),
+            dma((5,)),
+            dma((5,)),
+            dma((6, 6)),
+            dma((6, 6)),
+            dma((7,)),
+            dma((7,)),
+        ],
+        compiler_params=pltpu.CompilerParams(
+            collective_id=1, has_side_effects=True, vmem_limit_bytes=VMEM_LIMIT
+        ),
+        name="projection_gradients",
+    )(x, dmid, na, dp, att, gain, vec, w_qkv)
 
 
 def rms_scale(values):
@@ -180,27 +846,11 @@
         [piece.transpose(2, 0, 1, 3).reshape(rows_dev, q_width) for piece in out_fours], 0
     ).astype(jnp.bfloat16)
     mid = inputs + jnp.dot(attended_low, w_out, preferred_element_type=jnp.float32)
-    scale_ffn = rms_scale(mid)
-    normed_ffn = (mid * scale_ffn * norm_gain_ffn).astype(jnp.bfloat16)
-    gate_up = jnp.dot(normed_ffn, w_gate_up, preferred_element_type=jnp.float32)
-    gate = gate_up[:, :hidden_units]
-    upward = gate_up[:, hidden_units:]
-    sigma = jax.nn.sigmoid(gate)
-    hidden = (gate * sigma * upward).astype(jnp.bfloat16)
-    layer_out = mid + jnp.dot(hidden, w_down, preferred_element_type=jnp.float32)
-    grad_layer = cotangent[:, 0].reshape(all_rows, width).astype(jnp.float32)
-    grad_low = grad_layer.astype(jnp.bfloat16)
-    grad_down = contract_rows(hidden, grad_low)
-    grad_hidden = contract_cols(grad_low, w_down)
-    grad_gate = grad_hidden * upward * sigma * (1.0 + gate * (1.0 - sigma))
-    grad_upward = grad_hidden * gate * sigma
-    grad_gu_low = jnp.concatenate([grad_gate, grad_upward], -1).astype(jnp.bfloat16)
-    grad_gate_up = contract_rows(normed_ffn, grad_gu_low)
-    grad_nffn = contract_cols(grad_gu_low, w_gate_up)
-    grad_gain_ffn = jnp.sum(grad_nffn * mid * scale_ffn, axis=0)
-    grad_mid = grad_layer + rms_back(grad_nffn * norm_gain_ffn, mid, scale_ffn)
+    cot = cotangent[:, 0].reshape(all_rows, width)
+    layer_out, grad_mid, grad_gain_ffn, sum_gate_up, sum_down = ffn(
+        mid, cot, norm_gain_ffn[None], w_gate_up, w_down
+    )
     grad_mid_low = grad_mid.astype(jnp.bfloat16)
-    grad_out = contract_rows(attended_low, grad_mid_low)
     grad_attended = contract_cols(grad_mid_low, w_out).astype(jnp.bfloat16)
     query_grads = []
     key_grads = []
@@ -288,19 +938,34 @@
     grad_projected = jnp.concatenate([grad_proj_query, grad_proj_key, grad_values], -1).astype(
         jnp.bfloat16
     )
-    grad_qkv = contract_rows(normed_attn, grad_projected)
-    grad_nattn = contract_cols(grad_projected, w_qkv)
-    grad_gain_attn = jnp.sum(grad_nattn * inputs * scale_attn, axis=0)
-    grad_inputs = grad_mid + rms_back(grad_nattn * norm_gain_attn, inputs, scale_attn)
-    grad_qk = jnp.concatenate([grad_gain_query, grad_gain_key], 0)
+    vec = jnp.concatenate(
+        [
+            jnp.zeros((8, 128), f32),
+            grad_gain_ffn.reshape(8, 128),
+            jnp.concatenate([grad_gain_query, grad_gain_key], 0)[None],
+            jnp.zeros((7, 128), f32),
+        ],
+        0,
+    )
+    grad_inputs, sum_qkv, sum_out, vec = last_part(
+        tokens[:, 0].reshape(all_rows, width),
+        grad_mid,
+        normed_attn,
+        jnp.stack([grad_projected[:, :1024], grad_projected[:, 1024:]]),
+        attended_low,
+        norm_gain_attn[None],
+        vec,
+        w_qkv,
+    )
+    own = lax.axis_index("rows") * 8 + lax.axis_index("ctx")
     results = (
-        lax.psum_scatter(grad_gain_attn, ("rows", "ctx"), scatter_dimension=0, tiled=True),
-        lax.psum_scatter(grad_qkv, ("rows", "ctx"), scatter_dimension=0, tiled=True),
-        lax.psum_scatter(grad_qk, ("rows", "ctx"), scatter_dimension=0, tiled=True),
-        lax.psum_scatter(grad_out, ("rows", "ctx"), scatter_dimension=0, tiled=True),
-        lax.psum_scatter(grad_gain_ffn, ("rows", "ctx"), scatter_dimension=0, tiled=True),
-        lax.psum_scatter(grad_gate_up, ("rows", "ctx"), scatter_dimension=0, tiled=True),
-        lax.psum_scatter(grad_down, ("rows", "ctx"), scatter_dimension=0, tiled=True),
+        lax.dynamic_slice(vec[:8].reshape(1024), (own * 8,), (8,)),
+        sum_qkv,
+        lax.dynamic_slice(vec[16], (own,), (1,)),
+        sum_out,
+        lax.dynamic_slice(vec[8:16].reshape(1024), (own * 8,), (8,)),
+        sum_gate_up,
+        sum_down,
     )
     layer_shard = layer_out.astype(jnp.bfloat16).reshape(micro, 1, rows_dev, width)
     input_shard = grad_inputs.reshape(micro, 1, rows_dev, width)

time: 2490 us -> 548 us (0.22)
  waiting for transfers between devices: 1680 us -> 191 us
  blocking collectives: 453 us -> 0 us
  Pallas kernels: 0 us -> 137 us
  matrix products: 143 us -> 80.7 us
  starting transfers between devices: 41.2 us -> 0.32 us
    reduce_scatter x3 -> x0, waiting for transfers between devices: 1440 us -> none  [the longest x1 716 us: local(): lax.psum_scatter(grad_gate_up, ('rows', 'ctx'), scatter_dimension=0, tile...]
    unnamed x2 -> x0, blocking collectives: 453 us -> none
    pallas_call x0 -> x2, Pallas kernels: none -> 137 us  [the longest x1 91.6 us: ffn(): pl.pallas_call(ffn_kernel, out_shape=(jax.ShapeDtypeStruct((256, 1024), b...]
    dot_general x6 -> x0, matrix products: 53.8 us -> none  [the longest x4 36.4 us: contract_rows(): lax.dot_general(left, right, (((0,), (0,)), ((), ())), preferred_element_...]
    unnamed x13 -> x0, starting transfers between devices: 40.7 us -> none
    dot_general x4 -> x1, matrix products: 31.7 us -> 2.78 us  [contract_cols(): lax.dot_general(left, right, (((1,), (1,)), ((), ())), preferred_element_...]
    unnamed x96 -> x98, local copies, waits for them, and re-layouts: 40.6 us -> 15.5 us
  transfers between devices with their start and end apart: 24 -> 8, of which waited for: 11 -> 7; matrix products, arithmetic and copies ran while one was open for 21% -> 22% of each run, Pallas kernels for 0% -> 0%
where the time goes in v1:
time: 548 us; the launch traced here: 543 us
  waiting for transfers between devices  191 us (35%)
  Pallas kernels  137 us (25%)
  local copies, waits for them, and re-layouts  81.3 us (15%)
  matrix products  80.7 us (15%)
  other arithmetic  35.3 us (6%)
  between operations  15.5 us (3%)
    pallas_call x1, Pallas kernels, ffn(): pl.pallas_call(ffn_kernel, out_shape=(jax.ShapeDtypeStruct((256, 1024), b...  91.6 us
    reduce_scatter x2, waiting for transfers between devices, local(): lax.psum_scatter(grad_value_blocks.reshape(seq, k_width).astype(jnp.bfloa...  77.7 us
    all_gather x2, waiting for transfers between devices, local(): lax.all_gather(keys_local[lower:lower + rows_dev], 'ctx', axis=0, tiled=T...  54 us
    all_gather x2, waiting for transfers between devices, local(): lax.all_gather(values_local[lower:lower + rows_dev], 'ctx', axis=0, tiled...  50.1 us
    pallas_call x1, Pallas kernels, last_part(): pl.pallas_call(last_kernel, out_shape=(jax.ShapeDtypeStruct((256, 1024),...  45.8 us
    dot_general x8, matrix products, masked_scores(): jnp.einsum('kgqd,nkd->kgqn', query_four, key_block, preferred_element_typ...  18.8 us
    dot_general x4, matrix products, grad_step(): jnp.einsum('kgqn,kgqd->nkd', probs_low, grad_four, preferred_element_type...  16.5 us
    unnamed x98, local copies, waits for them, and re-layouts  15.5 us
  transfers between devices with their start and end apart: 8, of which 7 were waited for; matrix products, arithmetic and copies ran while one was open for 22% of the time, Pallas kernels for 0%

profile of v1, /device:TPU:1, one launch (start us, length us, event | category | flops | bytes accessed | tf_op | source)
XLA Modules:
  0.0 542.5 jit_solution(2991548274498645537)
XLA Ops:
  11.2 4.6 fusion.139
  25.5 29.0 %all-gather.5.cloned.1.call-done = bf16[1024,512]{0,1:T(8,128)(2,1)} async-done(((bf16[128,512]{0,1:T(8,128)(2,1)}), bf16[1024,512]{0,1:T(8,128)(2,1)}) %all-gather.5.cloned.1.call-update) | async-done | bytes 1048592 | tf_op jit(solution)/shard_map/all_gather | solution.py:804
  57.0 12.5 %while.78 = (s32[]{:T(128)}, f32[8,2,128]{2,1,0:T(2,128)S(1)}, f32[8,2,128]{2,1,0:T(2,128)S(1)}, s32[2,512]{1,0:T(2,128)S(1)}, s32[2,512]{1,0:T(2,128)S(1)}, /*i...) while((s32[]{:T(128)}, f32[8,2,128]{2,1,0:T(2,128)S(1)}, ...), condition=%wide.region_8.9_spmd.clone, body=%wide.region_5.8_spmd.clone.sunk | while | flops 142813312 | bytes 9492100 | solution.py:820
  60.1 3.2 select_reduce_fusion.4
  66.3 3.2 select_reduce_fusion.4
  69.6 26.5 %all-gather.7.cloned.1.call-done = bf16[1024,512]{1,0:T(8,128)(2,1)} async-done(((bf16[128,512]{1,0:T(8,128)(2,1)}), bf16[1024,512]{1,0:T(8,128)(2,1)}) %all-gather.7.cloned.1.call-update) | async-done | bytes 1048592 | tf_op jit(solution)/shard_map/all_gather | solution.py:805
  101.1 7.3 %while.79 = (s32[]{:T(128)}, f32[8,2,128,64]{2,3,1,0:T(8,128)}, s32[2,512]{1,0:T(2,128)S(1)}, s32[2,512]{1,0:T(2,128)S(1)}, s32[128]{0:T(128)S(1)}, /*index=5*/b...) while((s32[]{:T(128)}, f32[8,2,128,64]{2,3,1,0:T(8,128)}, ...), condition=%wide.region_10.11_spmd.clone, body=%wide.region_9.10_spmd.clone.sunk | while | flops 274137216 | bytes 2513543 | solution.py:836
  101.4 3.3 fusion.213
  104.9 3.5 fusion.213
  110.0 25.0 %all-gather.9.cloned.1.call-done = bf16[1024,512]{0,1:T(8,128)(2,1)} async-done(((bf16[128,512]{0,1:T(8,128)(2,1)}), bf16[1024,512]{0,1:T(8,128)(2,1)}) %all-gather.9.cloned.1.call-update) | async-done | bytes 1048592 | tf_op jit(solution)/shard_map/all_gather | solution.py:804
  138.1 14.8 %while.80 = (s32[]{:T(128)}, f32[8,2,128]{2,1,0:T(2,128)S(1)}, f32[8,2,128]{2,1,0:T(2,128)S(1)}, s32[2,512]{1,0:T(2,128)S(1)}, s32[2,512]{1,0:T(2,128)S(1)}, /*i...) while((s32[]{:T(128)}, f32[8,2,128]{2,1,0:T(2,128)S(1)}, ...), condition=%wide.region_16.17_spmd.clone, body=%wide.region_13.16_spmd.clone.sunk | while | flops 142813312 | bytes 9492608 | solution.py:820
  138.3 3.9 fusion.215
  142.2 3.2 select_reduce_fusion.5
  145.7 3.9 fusion.215
  149.6 3.2 select_reduce_fusion.5
  152.9 23.5 %all-gather.11.cloned.1.call-done = bf16[1024,512]{1,0:T(8,128)(2,1)} async-done(((bf16[128,512]{1,0:T(8,128)(2,1)}), bf16[1024,512]{1,0:T(8,128)(2,1)}) %all-gather.11.cloned.1.call-update) | async-done | bytes 1048592 | tf_op jit(solution)/shard_map/all_gather | solution.py:805
  181.6 6.5 %while.81 = (s32[]{:T(128)}, f32[8,2,128,64]{2,3,1,0:T(8,128)S(1)}, s32[2,512]{1,0:T(2,128)S(1)}, s32[2,512]{1,0:T(2,128)S(1)}, s32[128]{0:T(128)S(1)}, /*index=...) while((s32[]{:T(128)}, f32[8,2,128,64]{2,3,1,0:T(8,128)S(1)}, ...), condition=%wide.region_18.19_spmd.clone, body=%wide.region_17.18_spmd.clone.sunk | while | flops 274137216 | bytes 2513543 | solution.py:836
  181.8 3.0 fusion.221
  191.8 91.6 %feed_forward.1 = (bf16[256,1024]{1,0:T(8,128)(2,1)}, f32[256,1024]{1,0:T(8,128)}, f32[1,1024]{1,0:T(1,128)}, f32[8,9216]{1,0:T(8,128)}, f32[36,1024]{1,0:T(8,128)}) custom-call(f32[256,1024]{1,0:T(8,128)} %convolution_add_fusion.mid_ref, bf16[256,1024]{1,0:T(8,128)(2,1)} %bitcast.475, f32[1,1024]{1,0:T(1,128)} %bitcast.498, bf16[1024,9216]{1,0:T(8,128)(2,1)} %wgu_hbm.1, ...), custom_call_target="tpu_custom_call" | custom-call | tf_op jit(solution)/shard_map/feed_forward/pallas_call | solution.py:459
  289.4 23.5 %while.82 = (s32[]{:T(128)}, f32[8,2,128,64]{2,3,1,0:T(8,128)}, bf16[2,512,8,64]{1,3,2,0:T(8,128)(2,1)}, bf16[2,512,8,64]{1,3,2,0:T(8,128)(2,1)}, s32[2,512]{1,0...) while((s32[]{:T(128)}, f32[8,2,128,64]{2,3,1,0:T(8,128)}, ...), condition=%wide.region_21.22_spmd.clone, body=%wide.region_20.21_spmd.clone.sunk | while | flops 684523648 | bytes 47946528 | solution.py:905
  296.6 4.2 fusion.236
  308.7 4.1 fusion.236
  322.2 24.7 %while.83 = (s32[]{:T(128)}, f32[8,2,128,64]{2,3,1,0:T(8,128)S(1)}, bf16[2,512,8,64]{1,3,2,0:T(8,128)(2,1)}, bf16[2,512,8,64]{1,3,2,0:T(8,128)(2,1)}, s32[2,512]...) while((s32[]{:T(128)}, f32[8,2,128,64]{2,3,1,0:T(8,128)S(1)}, ...), condition=%wide.region_24.25_spmd.clone, body=%wide.region_23.24_spmd.clone.sunk | while | flops 684523648 | bytes 45850336 | solution.py:905
  330.4 4.1 fusion.251
  342.8 4.1 fusion.251
  351.7 2.9 copy.176
  369.2 4.1 reshape.290
  380.1 3.3 multiply_reduce_fusion
  384.9 7.9 %reduce-scatter.7.cloned.1.call-done = bf16[128,512]{1,0:T(8,128)(2,1)} async-done(((bf16[1024,512]{1,0:T(8,128)(2,1)}), bf16[128,512]{1,0:T(8,128)(2,1)}) %reduce-scatter.7.cloned.1.call-update) | async-done | bytes 131088 | tf_op jit(solution)/shard_map/reduce_scatter | solution.py:909
  396.5 36.7 %reduce-scatter.9.cloned.1.call-done = bf16[128,512]{1,0:T(8,128)(2,1)} async-done(((bf16[1024,512]{1,0:T(8,128)(2,1)}), bf16[128,512]{1,0:T(8,128)(2,1)}) %reduce-scatter.9.cloned.1.call-update) | async-done | bytes 131088 | tf_op jit(solution)/shard_map/reduce_scatter | solution.py:915
  433.2 41.0 %reduce-scatter.11.cloned.1.call-done = bf16[128,512]{1,0:T(8,128)(2,1)} async-done(((bf16[1024,512]{1,0:T(8,128)(2,1)}), bf16[128,512]{1,0:T(8,128)(2,1)}) %reduce-scatter.11.cloned.1.call-update) | async-done | bytes 131088 | tf_op jit(solution)/shard_map/reduce_scatter | solution.py:915
  477.0 45.8 %projection_gradients.1 = (f32[256,1024]{1,0:T(8,128)}, f32[8,2048]{1,0:T(8,128)}, f32[8,1024]{1,0:T(8,128)}, f32[24,128]{1,0:T(8,128)}) custom-call(bf16[256,1024]{1,0:T(8,128)(2,1)} %bitcast.457, f32[256,1024]{1,0:T(8,128)} %get-tuple-element.373.dmid_ref, bf16[256,1024]{1,0:T(8,128)(2,1)} %copy-done.15, bf16[2,256,1024]{2,1,0:T(8,128)(2,1)} %pad_maximum_fusion.2.dp_ref, ...), custom_call_target="tpu_custom_call" | custom-call | tf_op jit(solution)/shard_map/projection_gradients/pallas_call | solution.py:639
  (323 shorter events, 137.2 us)
Async XLA Ops:
  7.2 47.3 %all-gather.5.cloned.1.call-start = ((), (), s32[]{:S(2)}) async-start(), calls=%async_computation.4 | async-start | bytes 1179648 | tf_op jit(solution)/shard_map/all_gather | solution.py:804
  9.3 7.3 %copy-start.41 = (f32[64]{0:T(128)}, f32[64]{0:T(128)S(1)}, u32[]{:S(2)}) copy-start(f32[64]{0:T(128)S(1)} %get-tuple-element.1009) | copy-start | bytes 772
  9.3 14.7 %copy-start.43 = (f32[64]{0:T(128)}, f32[64]{0:T(128)S(1)}, u32[]{:S(2)}) copy-start(f32[64]{0:T(128)S(1)} %get-tuple-element.1008) | copy-start | bytes 772
  16.6 7.4 %copy-start.18 = (f32[256,64]{0,1:T(8,128)}, f32[256,64]{0,1:T(8,128)S(1)}, u32[]{:S(2)}) copy-start(f32[256,64]{0,1:T(8,128)S(1)} %get-tuple-element.1012) | copy-start | bytes 196612
  16.6 7.4 %copy-start.28 = (f32[256,64]{0,1:T(8,128)}, f32[256,64]{0,1:T(8,128)S(1)}, u32[]{:S(2)}) copy-start(f32[256,64]{0,1:T(8,128)S(1)} %get-tuple-element.1013) | copy-start | bytes 196612
  17.6 78.4 %all-gather.7.cloned.1.call-start = ((), (), s32[]{:S(2)}) async-start(), calls=%async_computation.5 | async-start | bytes 1179648 | tf_op jit(solution)/shard_map/all_gather | solution.py:805
  19.4 115.6 %all-gather.9.cloned.1.call-start = ((), (), s32[]{:S(2)}) async-start(), calls=%async_computation.6 | async-start | bytes 1179648 | tf_op jit(solution)/shard_map/all_gather | solution.py:804
  20.2 156.3 %all-gather.11.cloned.1.call-start = ((), (), s32[]{:S(2)}) async-start(), calls=%async_computation.7 | async-start | bytes 1179648 | tf_op jit(solution)/shard_map/all_gather | solution.py:805
  20.7 364.1 %reduce-scatter.5.cloned.1.call-start = ((), (), s32[]{:S(2)}) async-start(), calls=%async_computation.8 | async-start | bytes 1179648 | tf_op jit(solution)/shard_map/reduce_scatter | solution.py:909
  23.6 33.2 %copy-start.36 = (f32[256,16]{0,1:T(8,128)}, f32[256,16]{0,1:T(8,128)S(1)}, u32[]{:S(2)}) copy-start(f32[256,16]{0,1:T(8,128)S(1)} %add_rsqrt_fusion) | copy-start | bytes 49156
  108.4 29.7 %copy-start.2 = (bf16[2,512,8,64]{1,3,2,0:T(8,128)(2,1)}, bf16[2,512,8,64]{1,3,2,0:T(8,128)(2,1)S(1)}, u32[]{:S(2)}) copy-start(bf16[2,512,8,64]{1,3,2,0:T(8,128)(2,1)S(1)} %get-tuple-element.1709) | copy-start | bytes 3145732
  108.4 29.7 %copy-start.4 = (bf16[8,2,128,64]{2,3,1,0:T(8,128)(2,1)}, bf16[8,2,128,64]{2,3,1,0:T(8,128)(2,1)S(1)}, u32[]{:S(2)}) copy-start(bf16[8,2,128,64]{2,3,1,0:T(8,128)(2,1)S(1)} %get-tuple-element.1711) | copy-start | bytes 786436
  110.0 80.0 %copy-start.20 = (bf16[128,1024]{1,0:T(8,128)(2,1)}, bf16[128,1024]{1,0:T(8,128)(2,1)S(1)}, u32[]{:S(2)}) copy-start(bf16[128,1024]{1,0:T(8,128)(2,1)S(1)} %copy.119) | copy-start | bytes 786436
  152.9 28.6 %copy-start.24 = (f32[8,2,128,64]{2,3,1,0:T(8,128)S(1)}, f32[8,2,128,64]{2,3,1,0:T(8,128)}, u32[]{:S(2)}) copy-start(f32[8,2,128,64]{2,3,1,0:T(8,128)} %custom-call.5) | copy-start | bytes 1572868
  181.5 8.5 %copy-start.13 = (bf16[1024,1024]{1,0:T(8,128)(2,1)S(1)}, bf16[1024,1024]{1,0:T(8,128)(2,1)}, u32[]{:S(2)}) copy-start(bf16[1024,1024]{1,0:T(8,128)(2,1)} %param.30) | copy-start | bytes 6291460
  181.6 8.5 %copy-start.14 = (bf16[2,1,128,1024]{3,2,1,0:T(8,128)(2,1)S(1)}, bf16[2,1,128,1024]{3,2,1,0:T(8,128)(2,1)}, u32[]{:S(2)}) copy-start(bf16[2,1,128,1024]{3,2,1,0:T(8,128)(2,1)} %param.23) | copy-start | bytes 1572868
  283.4 6.0 %copy-start.3 = (bf16[2,512,8,64]{1,3,2,0:T(8,128)(2,1)S(1)}, bf16[2,512,8,64]{1,3,2,0:T(8,128)(2,1)}, u32[]{:S(2)}) copy-start(bf16[2,512,8,64]{1,3,2,0:T(8,128)(2,1)} %copy-done.2) | copy-start | bytes 3145732
  315.1 7.0 %copy-start.6 = (f32[8,2,128,64]{2,3,1,0:T(8,128)S(1)}, f32[8,2,128,64]{2,3,1,0:T(8,128)}, u32[]{:S(2)}) copy-start(f32[8,2,128,64]{2,3,1,0:T(8,128)} %custom-call.7) | copy-start | bytes 1572868
  319.9 72.9 %reduce-scatter.7.cloned.1.call-start = ((), (), s32[]{:S(2)}) async-start(), calls=%async_computation.9 | async-start | bytes 1179648 | tf_op jit(solution)/shard_map/reduce_scatter | solution.py:909
  351.6 81.6 %reduce-scatter.9.cloned.1.call-start = ((), (), s32[]{:S(2)}) async-start(), calls=%async_computation.10 | async-start | bytes 1179648 | tf_op jit(solution)/shard_map/reduce_scatter | solution.py:915
  356.6 7.4 %copy-start.44 = (f32[64]{0:T(128)S(1)}, f32[64]{0:T(128)}, u32[]{:S(2)}) copy-start(f32[64]{0:T(128)} %copy-done.43) | copy-start | bytes 772
  356.6 7.5 %copy-start.39 = (f32[256,8]{0,1:T(8,128)S(1)}, f32[256,8]{0,1:T(8,128)}, u32[]{:S(2)}) copy-start(f32[256,8]{0,1:T(8,128)} %copy-done.38) | copy-start | bytes 24580
  356.7 117.5 %reduce-scatter.11.cloned.1.call-start = ((), (), s32[]{:S(2)}) async-start(), calls=%async_computation.11 | async-start | bytes 1179648 | tf_op jit(solution)/shard_map/reduce_scatter | solution.py:915
  357.8 7.7 %copy-start.42 = (f32[64]{0:T(128)S(1)}, f32[64]{0:T(128)}, u32[]{:S(2)}) copy-start(f32[64]{0:T(128)} %copy-done.41) | copy-start | bytes 772
  357.8 8.9 %copy-start.17 = (bf16[2,512,8,64]{1,3,2,0:T(8,128)(2,1)S(1)}, bf16[2,512,8,64]{1,3,2,0:T(8,128)(2,1)}, u32[]{:S(2)}) copy-start(bf16[2,512,8,64]{1,3,2,0:T(8,128)(2,1)} %get-tuple-element.379) | copy-start | bytes 3145732
  364.4 8.9 %copy-start.7 = (f32[8,2,128,64]{2,3,1,0:T(8,128)S(1)}, f32[8,2,128,64]{2,3,1,0:T(8,128)}, u32[]{:S(2)}) copy-start(f32[8,2,128,64]{2,3,1,0:T(8,128)} %get-tuple-element.374) | copy-start | bytes 1572868
  364.4 8.9 %copy-start.29 = (f32[256,64]{0,1:T(8,128)S(1)}, f32[256,64]{0,1:T(8,128)}, u32[]{:S(2)}) copy-start(f32[256,64]{0,1:T(8,128)} %copy-done.28) | copy-start | bytes 196612
  383.4 10.8 %copy-start.11 = (f32[256,512]{0,1:T(8,128)S(1)}, f32[256,512]{0,1:T(8,128)}, u32[]{:S(2)}) copy-start(f32[256,512]{0,1:T(8,128)} %copy-done.10) | copy-start | bytes 1572868
  394.5 81.8 %copy-start.45 = (f32[1,1024]{1,0:T(1,128)S(1)}, f32[1,1024]{1,0:T(1,128)}, u32[]{:S(2)}) copy-start(f32[1,1024]{1,0:T(1,128)} %get-tuple-element.380) | copy-start | bytes 12292
  394.5 81.8 %copy-start.47 = (f32[24]{0:T(128)S(1)}, f32[24]{0:T(128)}, u32[]{:S(2)}) copy-start(f32[24]{0:T(128)} %pad.3.clone) | copy-start | bytes 292
  394.5 81.8 %copy-start.48 = (f32[24]{0:T(128)S(1)}, f32[24]{0:T(128)}, u32[]{:S(2)}) copy-start(f32[24]{0:T(128)} %pad.clone) | copy-start | bytes 292
  477.0 57.6 %copy-start.40 = (f32[36,1024]{1,0:T(8,128)S(1)}, f32[36,1024]{1,0:T(8,128)}, u32[]{:S(2)}) copy-start(f32[36,1024]{1,0:T(8,128)} %get-tuple-element.1699) | copy-start | bytes 442372
  (32 other events, 93.8 us)
Sparse Core Ops, SparseCore 0:
  17.8 36.7 all-gather.4
  56.2 39.8 all-gather.6
  97.7 37.3 all-gather.8
  136.6 39.8 all-gather.10
  320.1 32.4 reduce-scatter.4
  354.8 37.9 reduce-scatter.6
  395.2 37.9 reduce-scatter.8
  436.2 37.9 reduce-scatter.10

commit v2 on v1

--- a/solution.py
+++ b/solution.py
@@ -10,7 +10,6 @@
 MESH = pl.DeviceIdType.MESH
 norm_eps = 1e-05
 rope_theta = 1000000.0
-masked_score = -1e30
 f32 = jnp.float32
 bf16 = jnp.bfloat16
 VMEM_LIMIT = 64 * 2**20 - 2**18
@@ -505,6 +504,243 @@
     )(mid, cot, gain, w_gate_up, w_down)
 
 
+def lanes(rows):
+    return lax.broadcasted_iota(jnp.int32, (rows, 128), 1)
+
+
+def turn_heads(values):
+    low = lax.rem(lanes(values.shape[0]), 64) < 32
+    return jnp.where(low, pltpu.roll(values, 96, 1), pltpu.roll(values, 32, 1))
+
+
+def head_mean(values):
+    i = lax.broadcasted_iota(jnp.int32, (128, 128), 0)
+    j = lax.broadcasted_iota(jnp.int32, (128, 128), 1)
+    ones = jnp.where(lax.div(i, 64) == lax.div(j, 64), 1.0 / 64, 0.0).astype(bf16)
+    high = values.astype(bf16)
+    rest = (values - high.astype(f32)).astype(bf16)
+    return dot(high, ones) + dot(rest, ones)
+
+
+def gain_tiles(qk_gain):
+    swapped = pltpu.roll(qk_gain, 64, 1)
+    low = lax.broadcasted_iota(jnp.int32, (1, 128), 1) < 64
+    return jnp.where(low, qk_gain, swapped), jnp.where(low, swapped, qk_gain)
+
+
+def head_rows(values):
+    low = lanes(values.shape[0]) < 64
+    zero = jnp.zeros_like(values)
+    return jnp.concatenate([jnp.where(low, values, zero), jnp.where(low, zero, values)], 0)
+
+
+class Exchange:
+    def __init__(self, place, out, into, send_sems, recv_sems):
+        self.place = place
+        self.out = out
+        self.into = into
+        self.send_sems = send_sems
+        self.recv_sems = recv_sems
+
+    def copy(self, m, off):
+        j = lax.rem(self.place.ctx + off, 8)
+        return push(
+            self.place,
+            self.out.at[m, j],
+            self.into.at[m, self.place.ctx],
+            self.send_sems.at[m, off - 1],
+            self.recv_sems.at[m, off - 1],
+            (self.place.rows, j),
+        )
+
+    def send(self, m):
+        for off in range(1, 8):
+            self.copy(m, off).start()
+        self.into[m, self.place.ctx] = self.out[m, self.place.ctx]
+
+    def arrived(self, m):
+        for off in range(1, 8):
+            self.copy(m, off).wait_recv()
+
+    def sent(self):
+        for m in range(2):
+            for off in range(1, 8):
+                self.copy(m, off).wait_send()
+
+
+def ctx_peers(place):
+    return [(place.rows, lax.rem(place.ctx + off, 8)) for off in range(1, 8)]
+
+
+def document_edges(bounds_ref, m):
+    index = lax.broadcasted_iota(jnp.int32, (1, 1024), 1)
+    start = jnp.zeros((1, 1024), jnp.int32)
+    end = jnp.full((1, 1024), 1024, jnp.int32)
+    for k in range(1, 4):
+        cut = bounds_ref[m, 0, k]
+        start = jnp.where(index >= cut, cut, start)
+        end = jnp.where(index < bounds_ref[m, 0, 4 - k], bounds_ref[m, 0, 4 - k], end)
+    return start, end
+
+
+def attention_kernel(
+    bounds_ref,
+    x_ref,
+    cos_ref,
+    sin_ref,
+    gain_ref,
+    qk_gain_ref,
+    w_qkv_hbm,
+    w_out_hbm,
+    mid_ref,
+    na_ref,
+    att_ref,
+    proj_ref,
+    qkv_ref,
+    o_ref,
+    l_ref,
+    w_qkv,
+    w_out,
+    q_out,
+    a_out,
+    a_in,
+    q2,
+    kk,
+    vo,
+    w_sems,
+    q_send,
+    q_recv,
+    a_send,
+    a_recv,
+):
+    place = Place()
+    loads = [
+        pltpu.make_async_copy(w_qkv_hbm, w_qkv, w_sems.at[0]),
+        pltpu.make_async_copy(w_out_hbm, w_out, w_sems.at[1]),
+    ]
+    for load in loads:
+        load.start()
+    greet(ctx_peers(place))
+    heads_out = Exchange(place, q_out, qkv_ref, q_send, q_recv)
+    heads_back = Exchange(place, a_out, a_in, a_send, a_recv)
+
+    inputs = x_ref[...].astype(f32)
+    scale = lax.rsqrt(jnp.mean(inputs * inputs, axis=-1, keepdims=True) + norm_eps)
+    na_ref[...] = (inputs * scale * gain_ref[...]).astype(bf16)
+    loads[0].wait()
+    gain_q, gain_k = gain_tiles(qk_gain_ref[...])
+    low = lanes(256) < 64
+
+    def turned(tile, gain):
+        u = tile * lax.rsqrt(head_mean(tile * tile) + norm_eps) * gain
+        return u * cos_ref[...] + turn_heads(u) * sin_ref[...]
+
+    for i in range(4):
+        pair = dot(na_ref[...], w_qkv[:, pl.ds(256 * i, 256)])
+        proj_ref[:, pl.ds(256 * i, 256)] = pair
+        for j in range(2):
+            tile = turned(pair[:, 128 * j : 128 * j + 128], gain_q) * 0.125
+            for m in range(2):
+                q_out[m, 2 * i + j, :, pl.ds(0, 128)] = tile[128 * m : 128 * m + 128].astype(bf16)
+    for i in range(2):
+        key_pair = dot(na_ref[...], w_qkv[:, pl.ds(1024 + 256 * i, 256)])
+        value_pair = dot(na_ref[...], w_qkv[:, pl.ds(1536 + 256 * i, 256)])
+        proj_ref[:, pl.ds(1024 + 256 * i, 256)] = key_pair
+        for j in range(2):
+            key = turned(key_pair[:, 128 * j : 128 * j + 128], gain_k)
+            value = value_pair[:, 128 * j : 128 * j + 128]
+            first = jnp.where(low, key, pltpu.roll(value, 64, 1)).astype(bf16)
+            second = jnp.where(low, pltpu.roll(key, 64, 1), value).astype(bf16)
+            for m in range(2):
+                rows = slice(128 * m, 128 * m + 128)
+                q_out[m, 4 * i + 2 * j, :, pl.ds(128, 128)] = first[rows]
+                q_out[m, 4 * i + 2 * j + 1, :, pl.ds(128, 128)] = second[rows]
+    for m in range(2):
+        heads_out.send(m)
+
+    for m in range(2):
+        heads_out.arrived(m)
+        ends = document_edges(bounds_ref, m)[1]
+        for b in range(4):
+            query = qkv_ref[m, pl.ds(2 * b, 2), :, pl.ds(0, 128)].reshape(256, 128)
+            both = qkv_ref[m, pl.ds(2 * b, 2), :, pl.ds(128, 128)].reshape(256, 128).astype(f32)
+            swapped = pltpu.roll(both, 64, 1)
+            q2[b] = head_rows(query)
+            kk[b] = jnp.where(low, both, swapped).astype(bf16)
+            vo[b] = jnp.where(low, swapped, 1.0).astype(bf16)
+        for qb in range(4):
+            acc = jnp.zeros((512, 128), f32)
+            for kb in range(qb + 1):
+                scores = dot_cols(q2[qb], kk[kb])
+                t = 256 * qb + lax.rem(lax.broadcasted_iota(jnp.int32, (512, 256), 0), 256)
+                keep = t < ends[:, 256 * kb : 256 * kb + 256]
+                if kb == qb:
+                    s = 256 * kb + lax.broadcasted_iota(jnp.int32, (512, 256), 1)
+                    keep = keep & (s <= t)
+                weights = jnp.where(keep, jnp.exp(scores), 0.0).astype(bf16)
+                acc = acc + dot(weights, vo[kb])
+            total = pltpu.roll(acc, 64, 1)
+            head0 = acc[:256]
+            head1 = pltpu.roll(acc[256:], 64, 1)
+            denominator = jnp.where(low, total[:256], acc[256:])
+            out = jnp.where(low, head0, head1) / denominator
+            o_ref[m, pl.ds(256 * qb, 256), :] = out
+            log_total = jnp.log(denominator).T
+            l_ref[m, pl.ds(0, 1), pl.ds(256 * qb, 256)] = log_total[0:1]
+            l_ref[m, pl.ds(1, 1), pl.ds(256 * qb, 256)] = log_total[64:65]
+            for half in range(2):
+                a_out[m, 2 * qb + half] = out[128 * half : 128 * half + 128].astype(bf16)
+        heads_back.send(m)
+    loads[1].wait()
+    for m in range(2):
+        heads_back.arrived(m)
+        for j in range(8):
+            att_ref[pl.ds(128 * m, 128), pl.ds(128 * j, 128)] = a_in[m, j]
+    mid_ref[...] = x_ref[...].astype(f32) + dot(att_ref[...], w_out[...])
+    heads_out.sent()
+    heads_back.sent()
+
+
+def attention(bounds, x, cosine, sine, gain, qk_gain, w_qkv, w_out):
+    vmem = pl.BlockSpec(memory_space=pltpu.VMEM)
+    hbm = pl.BlockSpec(memory_space=pl.ANY)
+    smem = pl.BlockSpec(memory_space=pltpu.SMEM)
+    dma = pltpu.SemaphoreType.DMA
+    return pl.pallas_call(
+        attention_kernel,
+        out_shape=(
+            jax.ShapeDtypeStruct((256, 1024), f32),
+            jax.ShapeDtypeStruct((256, 1024), bf16),
+            jax.ShapeDtypeStruct((256, 1024), bf16),
+            jax.ShapeDtypeStruct((256, 1536), f32),
+            jax.ShapeDtypeStruct((2, 8, 128, 256), bf16),
+            jax.ShapeDtypeStruct((2, 1024, 128), f32),
+            jax.ShapeDtypeStruct((2, 2, 1024), f32),
+        ),
+        in_specs=[smem] + [vmem] * 5 + [hbm] * 2,
+        out_specs=(vmem,) * 7,
+        scratch_shapes=[
+            pltpu.VMEM((1024, 2048), bf16),
+            pltpu.VMEM((1024, 1024), bf16),
+            pltpu.VMEM((2, 8, 128, 256), bf16),
+            pltpu.VMEM((2, 8, 128, 128), bf16),
+            pltpu.VMEM((2, 8, 128, 128), bf16),
+            pltpu.VMEM((4, 512, 128), bf16),
+            pltpu.VMEM((4, 256, 128), bf16),
+            pltpu.VMEM((4, 256, 128), bf16),
+            dma((2,)),
+            dma((2, 7)),
+            dma((2, 7)),
+            dma((2, 7)),
+            dma((2, 7)),
+        ],
+        compiler_params=pltpu.CompilerParams(
+            collective_id=2, has_side_effects=True, vmem_limit_bytes=VMEM_LIMIT
+        ),
+        name="attention_forward",
+    )(bounds, x, cosine, sine, gain, qk_gain, w_qkv, w_out)
+
+
 def reorder_store(part, first, s, x_hi, at, width):
     part = part.reshape(4, 2, 8, 8, width)
     for y in range(4):
@@ -514,19 +750,41 @@
                 first[s, slot, :, at] = part[y, :, 4 * x_lo + z].reshape(16, width).astype(bf16)
 
 
-def last_kernel(
+def backward_kernel(
+    bounds_ref,
     x_ref,
+    cos_ref,
+    sin_ref,
+    gain_ref,
+    qk_gain_ref,
     dmid_ref,
     na_ref,
-    dp_ref,
     att_ref,
-    gain_ref,
+    proj_ref,
+    qkv_ref,
+    o_ref,
+    l_ref,
     vec_ref,
-    w_qkv,
+    w_qkv_hbm,
+    w_out_hbm,
     gtok_ref,
     gqkv_ref,
     gout_ref,
     vec_out,
+    w_qkv,
+    w_out,
+    do_out,
+    do_in,
+    g_out,
+    g_in,
+    q2,
+    do2,
+    kk,
+    vv,
+    kt,
+    delta,
+    dq,
+    dp,
     xin,
     dpin,
     dmin,
@@ -540,6 +798,11 @@
     q_in,
     vec,
     vec_in,
+    w_sems,
+    do_send,
+    do_recv,
+    g_send,
+    g_recv,
     x_send,
     x_recv,
     q_send,
@@ -550,47 +813,170 @@
     place = Place()
     core = place.core
     partner = place.partner()
-    greet([partner] + [place.neighbour(dim) for dim in range(6)])
+    loads = [
+        pltpu.make_async_copy(w_out_hbm, w_out, w_sems.at[0]),
+        pltpu.make_async_copy(w_qkv_hbm, w_qkv, w_sems.at[1]),
+    ]
+    for load in loads:
+        load.start()
+    greet([partner] + [place.neighbour(dim) for dim in range(6)] + ctx_peers(place))
     for half in range(2):
         dm_own[half] = dmid_ref[:, pl.ds(512 * half, 512)].astype(bf16)
     moves = [
         push(place, na_ref, xin.at[0], x_send.at[0], x_recv.at[0], partner),
         push(place, att_ref, xin.at[1], x_send.at[1], x_recv.at[1], partner),
-        push(place, dp_ref.at[1 - core], dpin, x_send.at[2], x_recv.at[2], partner),
-        push(place, dm_own.at[1 - core], dmin, x_send.at[3], x_recv.at[3], partner),
+        push(place, dm_own.at[1 - core], dmin, x_send.at[2], x_recv.at[2], partner),
     ]
     for move in moves:
         move.start()
+
+    grads_out = Exchange(place, do_out, do_in, do_send, do_recv)
+    grads_back = Exchange(place, g_out, g_in, g_send, g_recv)
+    loads[0].wait()
+    for i in range(4):
+        pair = dot_cols(dm_own[0], w_out[pl.ds(256 * i, 256), pl.ds(0, 512)]) + dot_cols(
+            dm_own[1], w_out[pl.ds(256 * i, 256), pl.ds(512, 512)]
+        )
+        for j in range(2):
+            for m in range(2):
+                do_out[m, 2 * i + j] = pair[
+                    128 * m : 128 * m + 128, 128 * j : 128 * j + 128
+                ].astype(bf16)
+    for m in range(2):
+        grads_out.send(m)
+
+    low = lanes(256) < 64
+    for m in range(2):
+        grads_out.arrived(m)
+        starts = document_edges(bounds_ref, m)[0]
+        for b in range(4):
+            query = qkv_ref[m, pl.ds(2 * b, 2), :, pl.ds(0, 128)].reshape(256, 128)
+            both = qkv_ref[m, pl.ds(2 * b, 2), :, pl.ds(128, 128)].reshape(256, 128).astype(f32)
+            grad = do_in[m, pl.ds(2 * b, 2)].reshape(256, 128)
+            swapped = pltpu.roll(both, 64, 1)
+            key_pair = jnp.where(low, both, swapped)
+            q2[b] = head_rows(query)
+            do2[b] = head_rows(grad)
+            kk[b] = key_pair.astype(bf16)
+            vv[b] = jnp.where(low, swapped, both).astype(bf16)
+            kt[b] = key_pair.T.astype(bf16)
+            inner = (grad.astype(f32) * o_ref[m, pl.ds(256 * b, 256), :]).T
+            delta[b, :, pl.ds(0, 256)] = jnp.sum(inner[:64], axis=0, keepdims=True)
+            delta[b, :, pl.ds(256, 256)] = jnp.sum(inner[64:], axis=0, keepdims=True)
+        for kb in range(4):
+            grad_key = jnp.zeros((256, 128), f32)
+            grad_value = jnp.zeros((256, 128), f32)
+            for qb in range(kb, 4):
+                scores = dot_cols(kk[kb], q2[qb])
+                log_total = jnp.concatenate(
+                    [l_ref[m, pl.ds(i, 1), pl.ds(256 * qb, 256)] for i in range(2)], 1
+                )
+                start = starts[:, 256 * qb : 256 * qb + 256]
+                s = 256 * kb + lax.broadcasted_iota(jnp.int32, (256, 512), 0)
+                keep = s >= jnp.concatenate([start, start], 1)
+                if kb == qb:
+                    t = 256 * qb + lax.rem(lax.broadcasted_iota(jnp.int32, (256, 512), 1), 256)
+                    keep = keep & (s <= t)
+                probs = jnp.where(keep, jnp.exp(scores - log_total), 0.0)
+                grad_probs = dot_cols(vv[kb], do2[qb])
+                grad_scores = (probs * (grad_probs - delta[qb])).astype(bf16)
+                grad_value = grad_value + dot(probs.astype(bf16), do2[qb])
+                grad_key = grad_key + dot(grad_scores, q2[qb])
+                grad_query = dot(kt[kb], grad_scores)
+                if kb == 0:
+                    dq[qb] = grad_query[:64]
+                else:
+                    dq[qb] = dq[qb] + grad_query[:64]
+            grad_key = grad_key + pltpu.roll(grad_key, 64, 1)
+            grad_value = grad_value + pltpu.roll(grad_value, 64, 1)
+            tile = jnp.where(low, grad_key, grad_value).astype(bf16)
+            for half in range(2):
+                g_out[m, 2 * kb + half, :, pl.ds(128, 128)] = tile[128 * half : 128 * half + 128]
+        for qb in range(4):
+            tile = (
+                (jnp.concatenate([dq[qb, :, pl.ds(0, 256)], dq[qb, :, pl.ds(256, 256)]], 0) * 0.125)
+                .T.astype(bf16)
+            )
+            for half in range(2):
+                g_out[m, 2 * qb + half, :, pl.ds(0, 128)] = tile[128 * half : 128 * half + 128]
+        grads_back.send(m)
+
     nat[:, pl.ds(0, 256)] = na_ref[...].T
     attt[:, pl.ds(0, 256)] = att_ref[...].T
-    cols[pl.ds(0, 256), pl.ds(0, 1024)] = dp_ref[core]
     cols[pl.ds(0, 256), pl.ds(1024, 512)] = dm_own[core]
     for move in moves:
         move.wait_recv()
     nat[:, pl.ds(256, 256)] = xin[0].T
     attt[:, pl.ds(256, 256)] = xin[1].T
-    cols[pl.ds(256, 256), pl.ds(0, 1024)] = dpin[...]
     cols[pl.ds(256, 256), pl.ds(1024, 512)] = dmin[...]
     quad = Scatter(place, q_first, q_held, q_send, q_recv, 4)
-    for s in range(6):
+
+    def projection_cols(s):
         left = nat if s < 4 else attt
         for x_hi in range(2):
             part = dot(left[pl.ds(512 * x_hi, 512), :], cols[:, pl.ds(256 * s, 256)])
             reorder_store(part, q_first, s, x_hi, slice(None), 256)
         quad.send(s, 0)
 
+    for s in range(4, 6):
+        projection_cols(s)
+
+    gain_q, gain_k = gain_tiles(qk_gain_ref[...])
+    for m in range(2):
+        grads_back.arrived(m)
+
+    def both_rows(j, at):
+        return jnp.concatenate([g_in[m, j, :, pl.ds(at, 128)] for m in range(2)], 0).astype(f32)
+
+    def head_back(grad, value, gain):
+        grad = grad * cos_ref[...] + turn_heads(grad * sin_ref[...])
+        scale = lax.rsqrt(head_mean(value * value) + norm_eps)
+        normed = value * scale
+        grad_e = grad * gain
+        gain_grad = jnp.sum(grad * normed, axis=0, keepdims=True)
+        return scale * (grad_e - normed * head_mean(grad_e * normed)), gain_grad
+
+    sum_q = jnp.zeros((1, 128), f32)
+    sum_k = jnp.zeros((1, 128), f32)
+    for j in range(8):
+        back, part = head_back(both_rows(j, 0), proj_ref[:, pl.ds(128 * j, 128)], gain_q)
+        dp[0, :, pl.ds(128 * j, 128)] = back.astype(bf16)
+        sum_q = sum_q + part
+    for i in range(4):
+        first = both_rows(2 * i, 128)
+        second = both_rows(2 * i + 1, 128)
+        grad_key = jnp.where(low, first, pltpu.roll(second, 64, 1))
+        grad_value = jnp.where(low, pltpu.roll(first, 64, 1), second)
+        back, part = head_back(grad_key, proj_ref[:, pl.ds(1024 + 128 * i, 128)], gain_k)
+        dp[1, :, pl.ds(128 * i, 128)] = back.astype(bf16)
+        dp[1, :, pl.ds(512 + 128 * i, 128)] = grad_value.astype(bf16)
+        sum_k = sum_k + part
+    move = push(place, dp.at[1 - core], dpin, x_send.at[3], x_recv.at[3], partner)
+    move.start()
+    moves.append(move)
+    sum_q = sum_q + pltpu.roll(sum_q, 64, 1)
+    sum_k = sum_k + pltpu.roll(sum_k, 64, 1)
+    vec[0, pl.ds(8, 8), :] = vec_ref[...]
+    vec[0, pl.ds(16, 8), :] = jnp.zeros((8, 128), f32)
+    vec[0, pl.ds(16, 1), :] = jnp.where(
+        lax.broadcasted_iota(jnp.int32, (1, 128), 1) < 64, sum_q, sum_k
+    )
+    cols[pl.ds(0, 256), pl.ds(0, 1024)] = dp[core]
+    move.wait_recv()
+    cols[pl.ds(256, 256), pl.ds(0, 1024)] = dpin[...]
+    for s in range(4):
+        projection_cols(s)
+
+    loads[1].wait()
     inputs = x_ref[...].astype(f32)
     scale = lax.rsqrt(jnp.mean(inputs * inputs, axis=-1, keepdims=True) + norm_eps)
     normed = inputs * scale
-    grad_n = dot_cols(dp_ref[0], w_qkv[:, pl.ds(0, 1024)]) + dot_cols(
-        dp_ref[1], w_qkv[:, pl.ds(1024, 1024)]
-    )
+    grad_n = dot_cols(dp[0], w_qkv[:, pl.ds(0, 1024)]) + dot_cols(dp[1], w_qkv[:, pl.ds(1024, 1024)])
     gain_grad = jnp.sum(grad_n * normed, axis=0, keepdims=True)
     grad_e = grad_n * gain_ref[...]
     gtok_ref[...] = dmid_ref[...] + scale * (
         grad_e - normed * jnp.mean(grad_e * normed, axis=-1, keepdims=True)
     )
-    vec[0, pl.ds(8, 16), :] = vec_ref[pl.ds(8, 16), :]
     for i in range(8):
         vec[0, pl.ds(i, 1), :] = gain_grad[:, 128 * i : 128 * i + 128]
 
@@ -631,22 +1017,40 @@
     for step in range(7):
         vec_move(step).wait_send()
     quad.sent()
-
-
-def last_part(x, dmid, na, dp, att, gain, vec, w_qkv):
+    grads_out.sent()
+    grads_back.sent()
+
+
+def backward(bounds, x, cosine, sine, gain, qk_gain, dmid, na, att, proj, qkv, o, l, vec, w_qkv, w_out):
     vmem = pl.BlockSpec(memory_space=pltpu.VMEM)
+    hbm = pl.BlockSpec(memory_space=pl.ANY)
+    smem = pl.BlockSpec(memory_space=pltpu.SMEM)
     dma = pltpu.SemaphoreType.DMA
     return pl.pallas_call(
-        last_kernel,
+        backward_kernel,
         out_shape=(
             jax.ShapeDtypeStruct((256, 1024), f32),
             jax.ShapeDtypeStruct((8, 2048), f32),
             jax.ShapeDtypeStruct((8, 1024), f32),
             jax.ShapeDtypeStruct((24, 128), f32),
         ),
-        in_specs=[vmem] * 8,
+        in_specs=[smem] + [vmem] * 13 + [hbm] * 2,
         out_specs=(vmem,) * 4,
         scratch_shapes=[
+            pltpu.VMEM((1024, 2048), bf16),
+            pltpu.VMEM((1024, 1024), bf16),
+            pltpu.VMEM((2, 8, 128, 128), bf16),
+            pltpu.VMEM((2, 8, 128, 128), bf16),
+            pltpu.VMEM((2, 8, 128, 256), bf16),
+            pltpu.VMEM((2, 8, 128, 256), bf16),
+            pltpu.VMEM((4, 512, 128), bf16),
+            pltpu.VMEM((4, 512, 128), bf16),
+            pltpu.VMEM((4, 256, 128), bf16),
+            pltpu.VMEM((4, 256, 128), bf16),
+            pltpu.VMEM((4, 128, 256), bf16),
+            pltpu.VMEM((4, 1, 512), f32),
+            pltpu.VMEM((4, 64, 512), f32),
+            pltpu.VMEM((2, 256, 1024), bf16),
             pltpu.VMEM((2, 256, 1024), bf16),
             pltpu.VMEM((256, 1024), bf16),
             pltpu.VMEM((256, 512), bf16),
@@ -660,6 +1064,11 @@
             pltpu.VMEM((6, 8, 256), f32),
             pltpu.VMEM((7, 24, 128), f32),
             pltpu.VMEM((7, 24, 128), f32),
+            dma((2,)),
+            dma((2, 7)),
+            dma((2, 7)),
+            dma((2, 7)),
+            dma((2, 7)),
             dma((5,)),
             dma((5,)),
             dma((6, 6)),
@@ -670,56 +1079,15 @@
         compiler_params=pltpu.CompilerParams(
             collective_id=1, has_side_effects=True, vmem_limit_bytes=VMEM_LIMIT
         ),
-        name="projection_gradients",
-    )(x, dmid, na, dp, att, gain, vec, w_qkv)
-
-
-def rms_scale(values):
-    return lax.rsqrt(jnp.mean(values * values, axis=-1, keepdims=True) + norm_eps)
-
-
-def rms_back(grad_normed, values, scale):
-    normed = values * scale
-    return scale * (grad_normed - normed * jnp.mean(grad_normed * normed, axis=-1, keepdims=True))
-
-
-def rotary_tables(positions, width):
-    half = width // 2
-    freqs = rope_theta ** (-2.0 * jnp.arange(half, dtype=jnp.float32) / width)
-    angles = positions.astype(jnp.float32)[:, None] * freqs[None, :]
-    cosine = jnp.cos(angles)
-    sine = jnp.sin(angles)
-    return (jnp.concatenate([cosine, cosine], -1), jnp.concatenate([sine, sine], -1))
-
-
-def rotate(values, cosine, sine):
-    half = values.shape[-1] // 2
-    turned = jnp.concatenate([-values[..., half:], values[..., :half]], -1)
-    return values * cosine[:, None, :] + turned * sine[:, None, :]
-
-
-def rotate_back(grads, cosine, sine):
-    half = grads.shape[-1] // 2
-    scaled = grads * sine[:, None, :]
-    turned = jnp.concatenate([scaled[..., half:], -scaled[..., :half]], -1)
-    return grads * cosine[:, None, :] + turned
-
-
-def document_of(index, bounds_row):
-    cuts = bounds_row[1:-1]
-    return jnp.sum((index[:, None] >= cuts[None, :]).astype(jnp.int32), axis=1)
-
-
-def contract_rows(left, right):
-    return lax.dot_general(
-        left, right, (((0,), (0,)), ((), ())), preferred_element_type=jnp.float32
-    )
-
-
-def contract_cols(left, right):
-    return lax.dot_general(
-        left, right, (((1,), (1,)), ((), ())), preferred_element_type=jnp.float32
-    )
+        name="attention_backward",
+    )(bounds, x, cosine, sine, gain, qk_gain, dmid, na, att, proj, qkv, o, l, vec, w_qkv, w_out)
+
+
+def tables(positions):
+    lane = jnp.arange(128, dtype=jnp.int32)
+    freqs = rope_theta ** (-2.0 * (lane % 32).astype(f32) / 64)
+    angles = positions.astype(f32)[:, None] * freqs[None, :]
+    return jnp.cos(angles), jnp.sin(angles) * jnp.where(lane % 64 < 32, -1.0, 1.0)
 
 
 def local(
@@ -735,230 +1103,37 @@
     w_gate_up,
     w_down,
 ):
-    micro = tokens.shape[0]
-    rows_dev = tokens.shape[2]
-    width = tokens.shape[3]
-    cycle = lax.axis_size("ctx")
-    seq = rows_dev * cycle
-    head_dim = qk_gain.shape[0] // 2
-    heads = w_out.shape[0] // head_dim
-    kv_heads = (w_qkv.shape[1] - heads * head_dim) // (2 * head_dim)
-    group = heads // kv_heads
-    hidden_units = w_down.shape[0]
-    q_width = heads * head_dim
-    k_width = kv_heads * head_dim
-    scale = head_dim ** (-0.5)
-    block = 512
-    blocks = seq // block
-    all_rows = micro * rows_dev
-    query_index = lax.axis_index("ctx") * rows_dev + jnp.arange(rows_dev, dtype=jnp.int32)
-    key_index = jnp.arange(seq, dtype=jnp.int32)
-    index_blocks = key_index.reshape(blocks, block)
-    gain_query = qk_gain[:head_dim]
-    gain_key = qk_gain[head_dim:]
-    inputs = tokens[:, 0].reshape(all_rows, width).astype(jnp.float32)
-    cosine, sine = rotary_tables(positions[:, 0].reshape(all_rows), head_dim)
-    scale_attn = rms_scale(inputs)
-    normed_attn = (inputs * scale_attn * norm_gain_attn).astype(jnp.bfloat16)
-    projected = jnp.dot(normed_attn, w_qkv, preferred_element_type=jnp.float32)
-    proj_query = projected[:, :q_width].reshape(all_rows, heads, head_dim)
-    proj_key = projected[:, q_width : q_width + k_width].reshape(all_rows, kv_heads, head_dim)
-    proj_value = projected[:, q_width + k_width :]
-    scale_query = rms_scale(proj_query)
-    scale_key = rms_scale(proj_key)
-    queries = rotate(proj_query * scale_query * gain_query, cosine, sine).astype(jnp.bfloat16)
-    keys_local = (
-        rotate(proj_key * scale_key * gain_key, cosine, sine)
-        .astype(jnp.bfloat16)
-        .reshape(all_rows, k_width)
+    x = tokens.reshape(256, 1024)
+    cot = cotangent.reshape(256, 1024)
+    cosine, sine = tables(positions.reshape(256))
+    mid, na, att, proj, qkv, o, l = attention(
+        bounds, x, cosine, sine, norm_gain_attn[None], qk_gain[None], w_qkv, w_out
     )
-    values_local = proj_value.astype(jnp.bfloat16)
-
-    def masked_scores(query_four, query_doc, key_block, index_block, doc_block):
-        scores = (
-            jnp.einsum("kgqd,nkd->kgqn", query_four, key_block, preferred_element_type=jnp.float32)
-            * scale
-        )
-        keep = (index_block[None, :] <= query_index[:, None]) & (
-            doc_block[None, :] == query_doc[:, None]
-        )
-        return (jnp.where(keep, scores, masked_score), keep)
-
-    query_fours = []
-    query_docs = []
-    doc_tables = []
-    log_totals = []
-    out_fours = []
-    kept_pairs = []
-    for step in range(micro):
-        lower = step * rows_dev
-        bounds_row = bounds[step, 0]
-        query_doc = document_of(query_index, bounds_row)
-        doc_blocks = document_of(key_index, bounds_row).reshape(blocks, block)
-        query_four = (
-            queries[lower : lower + rows_dev]
-            .reshape(rows_dev, kv_heads, group, head_dim)
-            .transpose(1, 2, 0, 3)
-        )
-        keys_all, values_all = (
-            lax.all_gather(keys_local[lower : lower + rows_dev], "ctx", axis=0, tiled=True),
-            lax.all_gather(values_local[lower : lower + rows_dev], "ctx", axis=0, tiled=True),
-        )
-        key_blocks = keys_all.reshape(blocks, block, kv_heads, head_dim)
-        value_blocks = values_all.reshape(blocks, block, kv_heads, head_dim)
-
-        def stats_step(carry, pieces):
-            top, total = carry
-            scores, keep = masked_scores(query_four, query_doc, pieces[0], pieces[1], pieces[2])
-            new_top = jnp.maximum(top, jnp.max(scores, axis=-1))
-            weights = jnp.where(keep, jnp.exp(scores - new_top[..., None]), 0.0)
-            total = total * jnp.exp(top - new_top) + jnp.sum(weights, axis=-1)
-            return ((new_top, total), None)
-
-        start_top = jnp.full((kv_heads, group, rows_dev), masked_score, jnp.float32)
-        start_total = jnp.zeros((kv_heads, group, rows_dev), jnp.float32)
-        (top, total), unused = lax.scan(
-            stats_step, (start_top, start_total), (key_blocks, index_blocks, doc_blocks)
-        )
-        log_total = top + jnp.log(total)
-
-        def output_step(carry, pieces):
-            scores, keep = masked_scores(query_four, query_doc, pieces[0], pieces[1], pieces[2])
-            probs = jnp.where(keep, jnp.exp(scores - log_total[..., None]), 0.0).astype(
-                jnp.bfloat16
-            )
-            carry = carry + jnp.einsum(
-                "kgqn,nkd->kgqd", probs, pieces[3], preferred_element_type=jnp.float32
-            )
-            return (carry, None)
-
-        start_out = jnp.zeros((kv_heads, group, rows_dev, head_dim), jnp.float32)
-        out_four, unused = lax.scan(
-            output_step, start_out, (key_blocks, index_blocks, doc_blocks, value_blocks)
-        )
-        query_fours.append(query_four)
-        query_docs.append(query_doc)
-        doc_tables.append(doc_blocks)
-        log_totals.append(log_total)
-        out_fours.append(out_four)
-        kept_pairs.append((keys_all, values_all))
-    attended_low = jnp.concatenate(
-        [piece.transpose(2, 0, 1, 3).reshape(rows_dev, q_width) for piece in out_fours], 0
-    ).astype(jnp.bfloat16)
-    mid = inputs + jnp.dot(attended_low, w_out, preferred_element_type=jnp.float32)
-    cot = cotangent[:, 0].reshape(all_rows, width)
-    layer_out, grad_mid, grad_gain_ffn, sum_gate_up, sum_down = ffn(
+    layer_out, dmid, gain_ffn, sum_gate_up, sum_down = ffn(
         mid, cot, norm_gain_ffn[None], w_gate_up, w_down
     )
-    grad_mid_low = grad_mid.astype(jnp.bfloat16)
-    grad_attended = contract_cols(grad_mid_low, w_out).astype(jnp.bfloat16)
-    query_grads = []
-    key_grads = []
-    value_grads = []
-    for step in range(micro):
-        lower = step * rows_dev
-        query_four = query_fours[step]
-        query_doc = query_docs[step]
-        doc_blocks = doc_tables[step]
-        log_total = log_totals[step]
-        grad_four = (
-            grad_attended[lower : lower + rows_dev]
-            .reshape(rows_dev, kv_heads, group, head_dim)
-            .transpose(1, 2, 0, 3)
-        )
-        delta = jnp.sum(grad_four.astype(jnp.float32) * out_fours[step], axis=-1)
-        back_keys, back_values = (
-            lax.all_gather(keys_local[lower : lower + rows_dev], "ctx", axis=0, tiled=True),
-            lax.all_gather(values_local[lower : lower + rows_dev], "ctx", axis=0, tiled=True),
-        )
-        back_key_blocks = back_keys.reshape(blocks, block, kv_heads, head_dim)
-        back_value_blocks = back_values.reshape(blocks, block, kv_heads, head_dim)
-
-        def grad_step(carry, pieces):
-            key_block, index_block, doc_block, value_block = pieces
-            scores, keep = masked_scores(query_four, query_doc, key_block, index_block, doc_block)
-            probs = jnp.where(keep, jnp.exp(scores - log_total[..., None]), 0.0)
-            probs_low = probs.astype(jnp.bfloat16)
-            grad_probs = jnp.einsum(
-                "kgqd,nkd->kgqn", grad_four, value_block, preferred_element_type=jnp.float32
-            )
-            grad_scores = (probs * (grad_probs - delta[..., None])).astype(jnp.bfloat16)
-            carry = (
-                carry
-                + jnp.einsum(
-                    "kgqn,nkd->kgqd", grad_scores, key_block, preferred_element_type=jnp.float32
-                )
-                * scale
-            )
-            grad_key_block = (
-                jnp.einsum(
-                    "kgqn,kgqd->nkd", grad_scores, query_four, preferred_element_type=jnp.float32
-                )
-                * scale
-            )
-            grad_value_block = jnp.einsum(
-                "kgqn,kgqd->nkd", probs_low, grad_four, preferred_element_type=jnp.float32
-            )
-            return (carry, (grad_key_block, grad_value_block))
-
-        start_grad = jnp.zeros((kv_heads, group, rows_dev, head_dim), jnp.float32)
-        grad_query_four, (grad_key_blocks, grad_value_blocks) = lax.scan(
-            grad_step, start_grad, (back_key_blocks, index_blocks, doc_blocks, back_value_blocks)
-        )
-        grad_keys, grad_values = (
-            lax.psum_scatter(
-                grad_key_blocks.reshape(seq, k_width).astype(jnp.bfloat16),
-                "ctx",
-                scatter_dimension=0,
-                tiled=True,
-            ).astype(jnp.float32),
-            lax.psum_scatter(
-                grad_value_blocks.reshape(seq, k_width).astype(jnp.bfloat16),
-                "ctx",
-                scatter_dimension=0,
-                tiled=True,
-            ).astype(jnp.float32),
-        )
-        query_grads.append(grad_query_four.transpose(2, 0, 1, 3).reshape(rows_dev, heads, head_dim))
-        key_grads.append(grad_keys)
-        value_grads.append(grad_values)
-    grad_query = jnp.concatenate(query_grads, 0)
-    grad_keys = jnp.concatenate(key_grads, 0).reshape(all_rows, kv_heads, head_dim)
-    grad_values = jnp.concatenate(value_grads, 0)
-    grad_turn_query = rotate_back(grad_query, cosine, sine)
-    grad_turn_key = rotate_back(grad_keys, cosine, sine)
-    grad_gain_query = jnp.sum(grad_turn_query * proj_query * scale_query, axis=(0, 1))
-    grad_gain_key = jnp.sum(grad_turn_key * proj_key * scale_key, axis=(0, 1))
-    grad_proj_query = rms_back(grad_turn_query * gain_query, proj_query, scale_query).reshape(
-        all_rows, q_width
-    )
-    grad_proj_key = rms_back(grad_turn_key * gain_key, proj_key, scale_key).reshape(
-        all_rows, k_width
-    )
-    grad_projected = jnp.concatenate([grad_proj_query, grad_proj_key, grad_values], -1).astype(
-        jnp.bfloat16
-    )
-    vec = jnp.concatenate(
-        [
-            jnp.zeros((8, 128), f32),
-            grad_gain_ffn.reshape(8, 128),
-            jnp.concatenate([grad_gain_query, grad_gain_key], 0)[None],
-            jnp.zeros((7, 128), f32),
-        ],
-        0,
-    )
-    grad_inputs, sum_qkv, sum_out, vec = last_part(
-        tokens[:, 0].reshape(all_rows, width),
-        grad_mid,
-        normed_attn,
-        jnp.stack([grad_projected[:, :1024], grad_projected[:, 1024:]]),
-        attended_low,
+    grad_tokens, sum_qkv, sum_out, vec = backward(
+        bounds,
+        x,
+        cosine,
+        sine,
         norm_gain_attn[None],
-        vec,
+        qk_gain[None],
+        dmid,
+        na,
+        att,
+        proj,
+        qkv,
+        o,
+        l,
+        gain_ffn.reshape(8, 128),
         w_qkv,
+        w_out,
     )
     own = lax.axis_index("rows") * 8 + lax.axis_index("ctx")
-    results = (
+    return (
+        layer_out.reshape(tokens.shape),
+        grad_tokens.reshape(tokens.shape),
         lax.dynamic_slice(vec[:8].reshape(1024), (own * 8,), (8,)),
         sum_qkv,
         lax.dynamic_slice(vec[16], (own,), (1,)),
@@ -966,19 +1141,6 @@
         lax.dynamic_slice(vec[8:16].reshape(1024), (own * 8,), (8,)),
         sum_gate_up,
         sum_down,
-    )
-    layer_shard = layer_out.astype(jnp.bfloat16).reshape(micro, 1, rows_dev, width)
-    input_shard = grad_inputs.reshape(micro, 1, rows_dev, width)
-    return (
-        layer_shard,
-        input_shard,
-        results[0],
-        results[1],
-        results[2],
-        results[3],
-        results[4],
-        results[5],
-        results[6],
     )
 
 

time: 548 us -> 206 us (0.38)
  waiting for transfers between devices: 191 us -> 0 us
  matrix products: 80.7 us -> 0 us
  local copies, waits for them, and re-layouts: 81.3 us -> 12.5 us
  Pallas kernels: 137 us -> 191 us
  other arithmetic: 35.3 us -> 1.93 us
  between operations: 15.5 us -> 0.69 us
    all_gather x4 -> x0, waiting for transfers between devices: 104 us -> none  [the longest x2 54 us: local(): lax.all_gather(keys_local[lower:lower + rows_dev], 'ctx', axis=0, tiled=T...]
    reduce_scatter x4 -> x0, waiting for transfers between devices: 85.6 us -> none  [the longest x2 77.7 us: local(): lax.psum_scatter(grad_value_blocks.reshape(seq, k_width).astype(jnp.bfloa...]
    dot_general x31 -> x0, matrix products: 80.7 us -> none  [the longest x8 18.8 us: masked_scores(): jnp.einsum('kgqd,nkd->kgqn', query_four, key_block, preferred_element_typ...]
    pallas_call x1 -> x2, Pallas kernels: 45.8 us -> 99.9 us  [the longest x1 67.2 us: backward(): pl.pallas_call(backward_kernel, out_shape=(jax.ShapeDtypeStruct((256, 102...]
    convert_element_type x8 -> x0, local copies, waits for them, and re-layouts: 21 us -> none  [the longest x4 11.6 us: local(): grad_value_blocks.reshape(seq, k_width).astype(jnp.bfloat16)]
    reduce_sum x16 -> x0, other arithmetic: 20.8 us -> none  [the longest x4 12.8 us: stats_step(): total = total * jnp.exp(top - new_top) + jnp.sum(weights, axis=-1)]
    mul x16 -> x0, local copies, waits for them, and re-layouts: 12.6 us -> none  [the longest x4 4.66 us: rotate(): return values * cosine[:, None, :] + turned * sine[:, None, :]]
    reshape x8 -> x0, local copies, waits for them, and re-layouts: 10.9 us -> none  [the longest x2 5.57 us: local(): value_blocks = values_all.reshape(blocks, block, kv_heads, head_dim)]
  transfers between devices with their start and end apart: 8 -> 0, of which waited for: 7 -> 0; matrix products, arithmetic and copies ran while one was open for 22% -> 0% of each run, Pallas kernels for 0% -> 0%
where the time goes in v2:
time: 206 us
  Pallas kernels  191 us (93%)
  local copies, waits for them, and re-layouts  12.5 us (6%)
    pallas_call x1, Pallas kernels, ffn(): pl.pallas_call(ffn_kernel, out_shape=(jax.ShapeDtypeStruct((256, 1024), b...  91 us
    pallas_call x1, Pallas kernels, backward(): pl.pallas_call(backward_kernel, out_shape=(jax.ShapeDtypeStruct((256, 102...  67.2 us
    pallas_call x1, Pallas kernels, attention(): pl.pallas_call(attention_kernel, out_shape=(jax.ShapeDtypeStruct((256, 10...  32.7 us
    unnamed x8, local copies, waits for them, and re-layouts  9.38 us

profile of v2, /device:TPU:1, one launch (start us, length us, event | category | flops | bytes accessed | tf_op | source)
XLA Modules:
  0.0 205.9 jit_solution(12680001257037040509)
XLA Ops:
  0.7 0.7 convert_element_type.17
  1.3 1.2 fusion
  2.6 32.7 %attention_forward.1 = (f32[256,1024]{1,0:T(8,128)}, bf16[256,1024]{1,0:T(8,128)(2,1)}, bf16[256,1024]{1,0:T(8,128)(2,1)}, f32[256,1536]{1,0:T(8,128)}, bf16[2,8...) custom-call(s32[2,1,5]{2,1,0:T(1,128)} %bounds_ref.3, bf16[256,1024]{1,0:T(8,128)(2,1)} %bitcast.18, ...), custom_call_target="tpu_custom_call" | custom-call | tf_op jit(solution)/shard_map/attention_forward/pallas_call | solution.py:709
  35.3 91.0 %feed_forward.1 = (bf16[256,1024]{1,0:T(8,128)(2,1)}, f32[256,1024]{1,0:T(8,128)}, f32[1,1024]{1,0:T(1,128)}, f32[8,9216]{1,0:T(8,128)}, f32[36,1024]{1,0:T(8,128)}) custom-call(f32[256,1024]{1,0:T(8,128)} %get-tuple-element.25.mid_ref, bf16[256,1024]{1,0:T(8,128)(2,1)} %bitcast.21, f32[1,1024]{1,0:T(1,128)} %bitcast.27, bf16[1024,9216]{1,0:T(8,128)(2,1)} %wgu_hbm.1, ...), custom_call_target="tpu_custom_call" | custom-call | tf_op jit(solution)/shard_map/feed_forward/pallas_call | solution.py:458
  126.3 0.0 copy-start
  126.3 67.2 %attention_backward.1 = (f32[256,1024]{1,0:T(8,128)}, f32[8,2048]{1,0:T(8,128)}, f32[8,1024]{1,0:T(8,128)}, f32[24,128]{1,0:T(8,128)}) custom-call(s32[2,1,5]{2,1,0:T(1,128)} %bounds_ref.3, bf16[256,1024]{1,0:T(8,128)(2,1)} %bitcast.19, f32[256,128]{1,0:T(8,128)} %get-tuple-element.53.cos_ref, f32[256,128]{1,0:T(8,128)} %get-tuple-element.52.sin_ref, ...), custom_call_target="tpu_custom_call" | custom-call | tf_op jit(solution)/shard_map/attention_backward/pallas_call | solution.py:1029
  193.4 0.7 slice_bitcast_fusion
  194.1 0.6 dynamic_slice.11
  194.7 0.6 dynamic_slice.14
  195.3 0.7 slice.10
  196.0 0.6 constant_dynamic-slice_fusion
  196.5 1.9 copy.28
  198.4 2.3 %copy.29 = f32[2,1,128,1024]{3,2,1,0:T(8,128)} copy(f32[2,1,128,1024]{3,2,1,0:T(8,128)} %bitcast.20) | data formatting | bytes 2097152
  200.7 1.5 copy.30
  202.2 1.4 copy.31
  203.6 1.7 copy.32
  205.3 0.0 copy-done
  205.3 0.7 copy.33
  (1 shorter events, 0.0 us)
Async XLA Ops:
  126.3 79.0 %copy-start = (f32[36,1024]{1,0:T(8,128)S(1)}, f32[36,1024]{1,0:T(8,128)}, u32[]{:S(2)}) copy-start(f32[36,1024]{1,0:T(8,128)} %get-tuple-element.73) | copy-start | bytes 442372

commit v3 on v2

v3 whole, which is shorter than its diff:
```python
import functools

import jax
import jax.numpy as jnp
from jax import lax
from jax.experimental import pallas as pl
from jax.experimental.pallas import tpu as pltpu
from jax.sharding import PartitionSpec as P

MESH = pl.DeviceIdType.MESH
norm_eps = 1e-05
rope_theta = 1000000.0
f32 = jnp.float32
bf16 = jnp.bfloat16
VMEM_LIMIT = 64 * 2**20 - 2**18


class Place:
    def __init__(self):
        r = lax.axis_index("rows")
        k = lax.axis_index("ctx")
        self.x_hi = lax.div(r, 8)
        self.y = lax.rem(lax.div(r, 2), 4)
        self.core = lax.rem(r, 2)
        self.x_lo = lax.div(k, 4)
        self.z = lax.rem(k, 4)
        self.rows = r
        self.ctx = k
        self.bits = [
            self.x_hi,
            lax.rem(self.x_hi + self.x_lo, 2),
            lax.div(self.y, 2),
            lax.rem(lax.div(self.y, 2) + lax.rem(self.y, 2), 2),
            lax.div(self.z, 2),
            lax.rem(lax.div(self.z, 2) + lax.rem(self.z, 2), 2),
        ]

    def at(self, x_hi=None, x_lo=None, y=None, z=None, core=None):
        x_hi = self.x_hi if x_hi is None else x_hi
        x_lo = self.x_lo if x_lo is None else x_lo
        y = self.y if y is None else y
        z = self.z if z is None else z
        core = self.core if core is None else core
        return (x_hi * 8 + y * 2 + core, x_lo * 4 + z)

    def partner(self):
        return self.at(core=1 - self.core)

    def neighbour(self, dim):
        if dim == 0:
            return self.at(x_hi=1 - self.x_hi, x_lo=1 - self.x_lo)
        if dim == 1:
            return self.at(x_lo=1 - self.x_lo)
        if dim == 2:
            return self.at(y=3 - self.y)
        if dim == 3:
            return self.at(y=self.y + 1 - 2 * lax.rem(self.y, 2))
        if dim == 4:
            return self.at(z=3 - self.z)
        return self.at(z=self.z + 1 - 2 * lax.rem(self.z, 2))


def gray(v):
    return v ^ (v >> 1)


def chip_number(x_hi, x_lo, y, z):
    return gray(2 * x_hi + x_lo) * 16 + gray(y) * 4 + gray(z)


def slot_of(number, s):
    turned = number << s
    return (turned & 63) | (turned >> 6)


HELD_AT = [64 - (64 >> t) for t in range(7)]


class Scatter:
    def __init__(self, place, first, held, send_sems, recv_sems, per):
        self.place = place
        self.first, self.first_cols = first
        self.held, self.held_cols = held
        self.send_sems = send_sems
        self.recv_sems = recv_sems
        self.per = per

    def part(self, s, t, which):
        half = 32 >> t
        if t == 0:
            return self.first, which * half, self.first_cols
        return self.held, HELD_AT[t - 1] + which * half, self.held_cols

    def copy(self, s, t):
        half = 32 >> t
        dim = (s + t) % 6
        ref, start, cols = self.part(s, t, 1 - self.place.bits[dim])
        return pltpu.make_async_remote_copy(
            src_ref=ref.at[s, pl.ds(start, half), :, cols],
            dst_ref=self.held.at[s, pl.ds(HELD_AT[t], half), :, self.held_cols],
            send_sem=self.send_sems.at[s, t],
            recv_sem=self.recv_sems.at[s, t],
            device_id=self.place.neighbour(dim),
            device_id_type=MESH,
        )

    def send(self, s, t):
        self.copy(s, t).start()

    def take(self, s, t):
        self.copy(s, t).wait_recv()
        half = 32 >> t
        ref, start, cols = self.part(s, t, self.place.bits[(s + t) % 6])
        per = min(self.per, half)

        def body(i, carry):
            for j in range(per):
                at = i * per + j
                self.held[s, HELD_AT[t] + at, :, self.held_cols] = (
                    self.held[s, HELD_AT[t] + at, :, self.held_cols].astype(f32)
                    + ref[s, start + at, :, cols].astype(f32)
                ).astype(bf16)
            return carry

        lax.fori_loop(0, half // per, body, 0)
        self.send(s, t + 1)

    def takes(self, t):
        for s in range(6):
            self.take(s, t)

    def last(self, s):
        self.copy(s, 5).wait_recv()
        ref, start, cols = self.part(s, 5, self.place.bits[(s + 5) % 6])
        return self.held[s, HELD_AT[5], :, self.held_cols].astype(f32) + ref[
            s, start, :, cols
        ].astype(f32)

    def sent(self, steps=range(6)):
        for s in range(6):
            for t in steps:
                self.copy(s, t).wait_send()


def greet(devices):
    barrier = pltpu.get_barrier_semaphore()
    for device in devices:
        pl.semaphore_signal(barrier, inc=1, device_id=device, device_id_type=MESH)
    pl.semaphore_wait(barrier, len(devices))


def greet_all(place, devices):
    barrier = pltpu.get_barrier_semaphore()
    targets = down_targets(place)
    for device in devices + targets[1:]:
        pl.semaphore_signal(barrier, inc=1, device_id=device, device_id_type=MESH)
    swapped = place.x_hi != place.core
    count = len(devices) + 3

    @pl.when(swapped)
    def _():
        pl.semaphore_signal(barrier, inc=1, device_id=targets[0], device_id_type=MESH)
        pl.semaphore_wait(barrier, count + 1)

    @pl.when(jnp.logical_not(swapped))
    def _():
        pl.semaphore_wait(barrier, count)


def push(place, src, dst, send_sem, recv_sem, device):
    return pltpu.make_async_remote_copy(
        src_ref=src,
        dst_ref=dst,
        send_sem=send_sem,
        recv_sem=recv_sem,
        device_id=device,
        device_id_type=MESH,
    )


def down_targets(place):
    return [
        place.at(x_hi=place.core, core=place.x_hi, z=lax.rem(place.z + off, 4)) for off in range(4)
    ]


def dot(left, right):
    return jnp.dot(left, right, preferred_element_type=f32)


def dot_cols(left, right):
    return lax.dot_general(left, right, (((1,), (1,)), ((), ())), preferred_element_type=f32)


FF_HALF = 2304


def finish_down(place, down, d_acc, d_stage, d_in, f_send, f_recv, gdn_ref):
    for s in range(6):
        d_acc[pl.ds(48 * (s // 2), 48), pl.ds(128 * (s % 2), 128)] = down.last(s)
    for z in range(4):
        d_stage[z, pl.ds(0, 36), :] = d_acc[pl.ds(36 * z, 36), :]
        d_stage[z, pl.ds(36, 4), :] = jnp.zeros((4, 256), f32)
    targets = down_targets(place)
    swapped = place.x_hi != place.core
    moves = []
    for off in range(4):
        moves.append(
            push(
                place,
                d_stage.at[lax.rem(place.z + off, 4)],
                d_in.at[place.z],
                f_send.at[off],
                f_recv.at[off],
                targets[off],
            )
        )
    for off in range(1, 4):
        moves[off].start()

    @pl.when(swapped)
    def _():
        moves[0].start()
        moves[0].wait_recv()

    @pl.when(jnp.logical_not(swapped))
    def _():
        d_in[place.z] = d_stage[place.z]

    for off in range(1, 4):
        moves[off].wait_recv()
    for z in range(4):
        gdn_ref[:, pl.ds(256 * z, 256)] = d_in[z, pl.ds(0, 36), :]
    for off in range(1, 4):
        moves[off].wait_send()

    @pl.when(swapped)
    def _():
        moves[0].wait_send()


def lanes(rows):
    return lax.broadcasted_iota(jnp.int32, (rows, 128), 1)


def turn_heads(values):
    low = lax.rem(lanes(values.shape[0]), 64) < 32
    return jnp.where(low, pltpu.roll(values, 96, 1), pltpu.roll(values, 32, 1))


def head_mean(values):
    i = lax.broadcasted_iota(jnp.int32, (128, 128), 0)
    j = lax.broadcasted_iota(jnp.int32, (128, 128), 1)
    ones = jnp.where(lax.div(i, 64) == lax.div(j, 64), 1.0 / 64, 0.0).astype(bf16)
    high = values.astype(bf16)
    rest = (values - high.astype(f32)).astype(bf16)
    return dot(high, ones) + dot(rest, ones)


def gain_tiles(qk_gain):
    swapped = pltpu.roll(qk_gain, 64, 1)
    low = lax.broadcasted_iota(jnp.int32, (1, 128), 1) < 64
    return jnp.where(low, qk_gain, swapped), jnp.where(low, swapped, qk_gain)


def head_rows(values):
    low = lanes(values.shape[0]) < 64
    zero = jnp.zeros_like(values)
    return jnp.concatenate([jnp.where(low, values, zero), jnp.where(low, zero, values)], 0)


class Exchange:
    def __init__(self, place, out, into_at, send_sems, recv_sems):
        self.place = place
        self.out = out
        self.into_at = into_at
        self.send_sems = send_sems
        self.recv_sems = recv_sems

    def copy(self, m, off):
        j = lax.rem(self.place.ctx + off, 8)
        return push(
            self.place,
            self.out.at[m, j],
            self.into_at(m, self.place.ctx),
            self.send_sems.at[m, off - 1],
            self.recv_sems.at[m, off - 1],
            (self.place.rows, j),
        )

    def send(self, m):
        for off in range(1, 8):
            self.copy(m, off).start()
        self.into_at(m, self.place.ctx)[...] = self.out[m, self.place.ctx]

    def arrived(self, m):
        for off in range(1, 8):
            self.copy(m, off).wait_recv()

    def sent(self):
        for m in range(2):
            for off in range(1, 8):
                self.copy(m, off).wait_send()


def ctx_peers(place):
    return [(place.rows, lax.rem(place.ctx + off, 8)) for off in range(1, 8)]


def document_edges(bounds_ref, m):
    index = lax.broadcasted_iota(jnp.int32, (1, 1024), 1)
    start = jnp.zeros((1, 1024), jnp.int32)
    end = jnp.full((1, 1024), 1024, jnp.int32)
    for k in range(1, 4):
        cut = bounds_ref[m, 0, k]
        start = jnp.where(index >= cut, cut, start)
        end = jnp.where(index < bounds_ref[m, 0, 4 - k], bounds_ref[m, 0, 4 - k], end)
    return start, end


def attention_kernel(
    bounds_ref,
    x_ref,
    cos_ref,
    sin_ref,
    gain_ref,
    qk_gain_ref,
    w_qkv_hbm,
    w_out_hbm,
    mid_ref,
    na_ref,
    att_ref,
    proj_ref,
    qkv_ref,
    o_ref,
    l_ref,
    w_qkv,
    w_out,
    q_out,
    a_out,
    a_in,
    q2,
    kk,
    vo,
    w_sems,
    q_send,
    q_recv,
    a_send,
    a_recv,
):
    place = Place()
    loads = [
        pltpu.make_async_copy(w_qkv_hbm, w_qkv, w_sems.at[0]),
        pltpu.make_async_copy(w_out_hbm, w_out, w_sems.at[1]),
    ]
    for load in loads:
        load.start()
    greet(ctx_peers(place))
    heads_out = Exchange(place, q_out, lambda m, j: qkv_ref.at[m, j], q_send, q_recv)
    heads_back = Exchange(place, a_out, lambda m, j: a_in.at[m, j], a_send, a_recv)

    inputs = x_ref[...].astype(f32)
    scale = lax.rsqrt(jnp.mean(inputs * inputs, axis=-1, keepdims=True) + norm_eps)
    na_ref[...] = (inputs * scale * gain_ref[...]).astype(bf16)
    loads[0].wait()
    gain_q, gain_k = gain_tiles(qk_gain_ref[...])
    low = lanes(256) < 64

    def turned(tile, gain):
        u = tile * lax.rsqrt(head_mean(tile * tile) + norm_eps) * gain
        return u * cos_ref[...] + turn_heads(u) * sin_ref[...]

    for i in range(4):
        pair = dot(na_ref[...], w_qkv[:, pl.ds(256 * i, 256)])
        proj_ref[:, pl.ds(256 * i, 256)] = pair
        for j in range(2):
            tile = turned(pair[:, 128 * j : 128 * j + 128], gain_q) * 0.125
            for m in range(2):
                q_out[m, 2 * i + j, :, pl.ds(0, 128)] = tile[128 * m : 128 * m + 128].astype(bf16)
    for i in range(2):
        key_pair = dot(na_ref[...], w_qkv[:, pl.ds(1024 + 256 * i, 256)])
        value_pair = dot(na_ref[...], w_qkv[:, pl.ds(1536 + 256 * i, 256)])
        proj_ref[:, pl.ds(1024 + 256 * i, 256)] = key_pair
        for j in range(2):
            key = turned(key_pair[:, 128 * j : 128 * j + 128], gain_k)
            value = value_pair[:, 128 * j : 128 * j + 128]
            first = jnp.where(low, key, pltpu.roll(value, 64, 1)).astype(bf16)
            second = jnp.where(low, pltpu.roll(key, 64, 1), value).astype(bf16)
            for m in range(2):
                rows = slice(128 * m, 128 * m + 128)
                q_out[m, 4 * i + 2 * j, :, pl.ds(128, 128)] = first[rows]
                q_out[m, 4 * i + 2 * j + 1, :, pl.ds(128, 128)] = second[rows]
    for m in range(2):
        heads_out.send(m)

    for m in range(2):
        heads_out.arrived(m)
        ends = document_edges(bounds_ref, m)[1]
        for b in range(4):
            query = qkv_ref[m, pl.ds(2 * b, 2), :, pl.ds(0, 128)].reshape(256, 128)
            both = qkv_ref[m, pl.ds(2 * b, 2), :, pl.ds(128, 128)].reshape(256, 128).astype(f32)
            swapped = pltpu.roll(both, 64, 1)
            q2[b] = head_rows(query)
            kk[b] = jnp.where(low, both, swapped).astype(bf16)
            vo[b] = jnp.where(low, swapped, 1.0).astype(bf16)
        for qb in range(4):
            acc = jnp.zeros((512, 128), f32)
            for kb in range(qb + 1):
                scores = dot_cols(q2[qb], kk[kb])
                t = 256 * qb + lax.rem(lax.broadcasted_iota(jnp.int32, (512, 256), 0), 256)
                keep = t < ends[:, 256 * kb : 256 * kb + 256]
                if kb == qb:
                    s = 256 * kb + lax.broadcasted_iota(jnp.int32, (512, 256), 1)
                    keep = keep & (s <= t)
                weights = jnp.where(keep, jnp.exp(scores), 0.0).astype(bf16)
                acc = acc + dot(weights, vo[kb])
            total = pltpu.roll(acc, 64, 1)
            head0 = acc[:256]
            head1 = pltpu.roll(acc[256:], 64, 1)
            denominator = jnp.where(low, total[:256], acc[256:])
            out = jnp.where(low, head0, head1) / denominator
            o_ref[m, pl.ds(256 * qb, 256), :] = out
            log_total = jnp.log(denominator).T
            l_ref[m, pl.ds(0, 1), pl.ds(256 * qb, 256)] = log_total[0:1]
            l_ref[m, pl.ds(1, 1), pl.ds(256 * qb, 256)] = log_total[64:65]
            for half in range(2):
                a_out[m, 2 * qb + half] = out[128 * half : 128 * half + 128].astype(bf16)
        heads_back.send(m)
    loads[1].wait()
    for m in range(2):
        heads_back.arrived(m)
        for j in range(8):
            att_ref[pl.ds(128 * m, 128), pl.ds(128 * j, 128)] = a_in[m, j]
    mid_ref[...] = x_ref[...].astype(f32) + dot(att_ref[...], w_out[...])
    heads_out.sent()
    heads_back.sent()


def attention(bounds, x, cosine, sine, gain, qk_gain, w_qkv, w_out):
    vmem = pl.BlockSpec(memory_space=pltpu.VMEM)
    hbm = pl.BlockSpec(memory_space=pl.ANY)
    smem = pl.BlockSpec(memory_space=pltpu.SMEM)
    dma = pltpu.SemaphoreType.DMA
    return pl.pallas_call(
        attention_kernel,
        out_shape=(
            jax.ShapeDtypeStruct((256, 1024), f32),
            jax.ShapeDtypeStruct((256, 1024), bf16),
            jax.ShapeDtypeStruct((256, 1024), bf16),
            jax.ShapeDtypeStruct((256, 1536), f32),
            jax.ShapeDtypeStruct((2, 8, 128, 256), bf16),
            jax.ShapeDtypeStruct((2, 1024, 128), f32),
            jax.ShapeDtypeStruct((2, 2, 1024), f32),
        ),
        in_specs=[smem] + [vmem] * 5 + [hbm] * 2,
        out_specs=(vmem,) * 7,
        scratch_shapes=[
            pltpu.VMEM((1024, 2048), bf16),
            pltpu.VMEM((1024, 1024), bf16),
            pltpu.VMEM((2, 8, 128, 256), bf16),
            pltpu.VMEM((2, 8, 128, 128), bf16),
            pltpu.VMEM((2, 8, 128, 128), bf16),
            pltpu.VMEM((4, 512, 128), bf16),
            pltpu.VMEM((4, 256, 128), bf16),
            pltpu.VMEM((4, 256, 128), bf16),
            dma((2,)),
            dma((2, 7)),
            dma((2, 7)),
            dma((2, 7)),
            dma((2, 7)),
        ],
        compiler_params=pltpu.CompilerParams(
            collective_id=2, has_side_effects=True, vmem_limit_bytes=VMEM_LIMIT
        ),
        name="attention_forward",
    )(bounds, x, cosine, sine, gain, qk_gain, w_qkv, w_out)


def reorder_store(part, first, s, x_hi, at, width):
    part = part.reshape(4, 2, 8, 8, width)
    for y in range(4):
        for x_lo in range(2):
            for z in range(4):
                slot = slot_of(chip_number(x_hi, x_lo, y, z), s)
                first[s, slot, :, at] = part[y, :, 4 * x_lo + z].reshape(16, width).astype(bf16)


def main_kernel(
    bounds_ref,
    mid_ref,
    gain_ffn_ref,
    gain_ref,
    qk_gain_ref,
    cot_hbm,
    x_hbm,
    cos_hbm,
    sin_hbm,
    na_hbm,
    att_hbm,
    proj_hbm,
    qkv_hbm,
    o_hbm,
    l_hbm,
    wgu_hbm,
    wd_hbm,
    w_qkv_hbm,
    w_out_hbm,
    out_hbm,
    gtok_hbm,
    ggu_ref,
    gdn_ref,
    gqkv_ref,
    gout_ref,
    vec_out,
    g_first,
    g_held,
    d_first,
    d_held,
    nf,
    dyb,
    sum_send,
    sum_recv,
    xboth,
    dmid,
    do_out,
    do_in,
    dpin,
    dmin,
    dm_own,
    g_fin,
    g_in,
    d_acc,
    d_stage,
    d_in,
    q_fin,
    q_in,
    vec,
    vec_in,
    w_sems,
    l_sems,
    x_send,
    x_recv,
    g_send,
    g_recv,
    d_send,
    d_recv,
    q_send,
    q_recv,
    f_send,
    f_recv,
    do_send,
    do_recv,
    t_send,
    t_recv,
    v_send,
    v_recv,
    free_sem,
):
    place = Place()
    core = place.core
    partner = place.partner()
    every = slice(None)
    down = Scatter(place, (d_first, every), (d_held, every), d_send, d_recv, 4)
    both = Scatter(place, (g_first, every), (g_held, every), g_send, g_recv, 2)
    quad = Scatter(
        place, (g_first, pl.ds(0, 256)), (g_first, pl.ds(256, 256)), q_send, q_recv, 4
    )
    def t_at(m, j):
        return nf.at[
            pl.ds(pl.multiple_of(256 * m + 128 * lax.div(j, 4), 128), 128),
            pl.ds(pl.multiple_of(256 * lax.rem(j, 4), 256), 256),
        ]

    grads_out = Exchange(place, do_out, lambda m, j: do_in.at[m, j], do_send, do_recv)
    own_rows = pl.ds(0, 256)
    other_rows = pl.ds(256, 256)
    to_dy = push(place, cot_hbm, dyb.at[other_rows], x_send.at[0], x_recv.at[0], partner)
    to_nf = push(place, nf.at[own_rows], nf.at[other_rows], x_send.at[1], x_recv.at[1], partner)
    to_out = push(place, sum_send, sum_recv.at[0], x_send.at[2], x_recv.at[2], partner)
    to_back = push(place, sum_send, sum_recv.at[1], x_send.at[3], x_recv.at[3], partner)
    to_na = push(place, na_hbm, xboth.at[0], x_send.at[4], x_recv.at[4], partner)
    to_att = push(place, att_hbm, xboth.at[1], x_send.at[5], x_recv.at[5], partner)
    to_dm = push(place, dm_own.at[1 - core], dmin, x_send.at[6], x_recv.at[6], partner)
    out_copy = pltpu.make_async_copy(sum_send, out_hbm, l_sems.at[0])

    def feed_forward(wgu, wd, nft, h, ht, dgu, sum_own):
        loads = []
        for i in range(3):
            at = pl.multiple_of(core * FF_HALF + 768 * i, 256)
            up_at = pl.multiple_of(4608 + core * FF_HALF + 768 * i, 256)
            loads.append(
                [
                    pltpu.make_async_copy(
                        wgu_hbm.at[:, pl.ds(at, 768)],
                        wgu.at[:, pl.ds(768 * i, 768)],
                        w_sems.at[3 * i],
                    ),
                    pltpu.make_async_copy(
                        wgu_hbm.at[:, pl.ds(up_at, 768)],
                        wgu.at[:, pl.ds(FF_HALF + 768 * i, 768)],
                        w_sems.at[3 * i + 1],
                    ),
                    pltpu.make_async_copy(
                        wd_hbm.at[pl.ds(at, 768)], wd.at[pl.ds(768 * i, 768)], w_sems.at[3 * i + 2]
                    ),
                ]
            )
        cot_load = pltpu.make_async_copy(cot_hbm, dyb.at[own_rows], l_sems.at[1])
        cot_load.start()
        for copies in loads:
            for copy in copies:
                copy.start()
        greet_all(
            place,
            [partner] + [place.neighbour(dim) for dim in range(6)] + ctx_peers(place),
        )
        to_dy.start()
        mid = mid_ref[...]
        scale = lax.rsqrt(jnp.mean(mid * mid, axis=-1, keepdims=True) + norm_eps)
        nf[own_rows, :] = (mid * scale * gain_ffn_ref[...]).astype(bf16)
        to_nf.start()
        nft[:, own_rows] = nf[own_rows, :].T
        to_na.start()
        to_att.start()
        cot_load.wait()
        to_dy.wait_recv()
        to_nf.wait_recv()
        nft[:, other_rows] = nf[other_rows, :].T

        for i in range(3):
            for copy in loads[i]:
                copy.wait()

            def units(j, carry, i=i):
                at = pl.multiple_of(768 * i + 256 * j, 256)
                up_at = pl.multiple_of(FF_HALF + 768 * i + 256 * j, 256)
                gate = dot(nf[...], wgu[:, pl.ds(at, 256)])
                upward = dot(nf[...], wgu[:, pl.ds(up_at, 256)])
                grad_hidden = dot_cols(dyb[...], wd[pl.ds(at, 256), :])
                sigma = 1.0 / (1.0 + jnp.exp(-gate))
                silu = gate * sigma
                h[:, pl.ds(at, 256)] = (silu * upward).astype(bf16)
                dgu[:, pl.ds(at, 256)] = (
                    grad_hidden * upward * (sigma + silu * (1.0 - sigma))
                ).astype(bf16)
                dgu[:, pl.ds(up_at, 256)] = (grad_hidden * silu).astype(bf16)
                return carry

            lax.fori_loop(0, 3, units, 0)

        for block in range(3):
            ht[...] = h[:, pl.ds(768 * block, 768)].T

            def down_cols(z, carry, block=block):
                part = dot(ht[...], dyb[:, pl.ds(pl.multiple_of(256 * z, 256), 256)])
                z_number = 2 * lax.div(z, 2) + lax.rem(lax.div(z, 2) + lax.rem(z, 2), 2)
                for i in range(16):
                    q = 16 * block + i
                    y, core_to, x_lo, rg = q // 12, (q // 6) % 2, (q // 3) % 2, q % 3
                    number = chip_number(core_to, x_lo, y, 0) + z_number
                    for ch in range(2):
                        s = 2 * rg + ch
                        turned = number * (1 << s)
                        slot = lax.rem(turned, 64) + lax.div(turned, 64)
                        d_first[s, slot] = part[
                            48 * i : 48 * i + 48, 128 * ch : 128 * ch + 128
                        ].astype(bf16)
                return carry

            lax.fori_loop(0, 4, down_cols, 0)
        for s in range(6):
            down.send(s, 0)

        def back_cols(j, carry):
            at = pl.ds(pl.multiple_of(256 * j, 256), 256)
            part = dot_cols(dgu[...], wgu[at, :])
            dmid[:, at] = part[:256]
            sum_send[:, at] = part[256:].astype(bf16)
            return carry

        lax.fori_loop(0, 4, back_cols, 0)
        to_back.start()

        def gate_up(s):
            def gate_cols(j, carry):
                at = pl.ds(pl.multiple_of(256 * j, 256), 256)
                cols = dgu[:, pl.ds(pl.multiple_of(768 * s + 256 * j, 256), 256)]
                for x_hi in range(2):
                    part = dot(nft[pl.ds(512 * x_hi, 512), :], cols)
                    reorder_store(part, g_first, s, x_hi, at, 256)
                return carry

            lax.fori_loop(0, 3, gate_cols, 0)
            both.send(s, 0)

        for s in range(2):
            gate_up(s)

        to_back.wait_send()

        def out_cols(j, carry):
            at = pl.ds(pl.multiple_of(256 * j, 256), 256)
            part = dot(h[...], wd[:, at])
            sum_own[:, at] = part[:256]
            sum_send[:, at] = part[256:].astype(bf16)
            return carry

        lax.fori_loop(0, 4, out_cols, 0)
        to_out.start()
        w_out = wd.at[pl.ds(0, 1024)]
        w_out_load = pltpu.make_async_copy(w_out_hbm, w_out, l_sems.at[4])
        w_out_load.start()

        to_back.wait_recv()
        mid = mid_ref[...]
        scale = lax.rsqrt(jnp.mean(mid * mid, axis=-1, keepdims=True) + norm_eps)
        normed = mid * scale
        grad_nffn = dmid[...] + sum_recv[1].astype(f32)
        gain_grad = jnp.sum(grad_nffn * normed, axis=0, keepdims=True)
        for i in range(8):
            vec[0, pl.ds(8 + i, 1), :] = gain_grad[:, 128 * i : 128 * i + 128]
        grad_e = grad_nffn * gain_ffn_ref[...]
        dmid[...] = dyb[own_rows, :].astype(f32) + scale * (
            grad_e - normed * jnp.mean(grad_e * normed, axis=-1, keepdims=True)
        )
        for half in range(2):
            dm_own[half] = dmid[:, pl.ds(512 * half, 512)].astype(bf16)
        to_dm.start()

        to_nf.wait_send()
        w_out_load.wait()
        for i in range(4):
            pair = dot_cols(dm_own[0], wd[pl.ds(256 * i, 256), pl.ds(0, 512)]) + dot_cols(
                dm_own[1], wd[pl.ds(256 * i, 256), pl.ds(512, 512)]
            )
            for j in range(2):
                for m in range(2):
                    do_out[m, 2 * i + j] = pair[
                        128 * m : 128 * m + 128, 128 * j : 128 * j + 128
                    ].astype(bf16)
        for m in range(2):
            grads_out.send(m)
        for s in range(2, 6):
            gate_up(s)
        to_out.wait()
        sum_send[...] = (mid_ref[...] + sum_own[...] + sum_recv[0].astype(f32)).astype(bf16)
        out_copy.start()

    pl.run_scoped(
        feed_forward,
        pltpu.VMEM((1024, 4608), bf16),
        pltpu.VMEM((FF_HALF, 1024), bf16),
        pltpu.VMEM((1024, 512), bf16),
        pltpu.VMEM((512, FF_HALF), bf16),
        pltpu.VMEM((768, 512), bf16),
        pltpu.VMEM((512, 4608), bf16),
        pltpu.VMEM((256, 1024), f32),
    )

    def attention_back(
        w_qkv, x_ref, gtok, cos_ref, sin_ref, proj_ref, qkv_ref, o_ref, l_ref,
        q2, do2, kk, vv, kt, delta, dq, dp, own, nat, attt, cols, t_out,
    ):
        sources = [qkv_hbm, o_hbm, l_hbm, cos_hbm, sin_hbm, proj_hbm, x_hbm, w_qkv_hbm]
        loads = [
            pltpu.make_async_copy(source, target, w_sems.at[i])
            for i, (source, target) in enumerate(
                zip(
                    sources,
                    [qkv_ref, o_ref, l_ref, cos_ref, sin_ref, proj_ref, x_ref, w_qkv],
                    strict=True,
                )
            )
        ]
        for load in loads:
            load.start()
        grads_back = Exchange(place, t_out, t_at, t_send, t_recv)
        down.takes(0)
        for load in loads[:3]:
            load.wait()
        low = lanes(256) < 64

        def heads_back(m):
            grads_out.arrived(m)
            starts = document_edges(bounds_ref, m)[0]
            for b in range(4):
                query = qkv_ref[m, pl.ds(2 * b, 2), :, pl.ds(0, 128)].reshape(256, 128)
                pair = qkv_ref[m, pl.ds(2 * b, 2), :, pl.ds(128, 128)].reshape(256, 128)
                pair = pair.astype(f32)
                grad = do_in[m, pl.ds(2 * b, 2)].reshape(256, 128)
                swapped = pltpu.roll(pair, 64, 1)
                key_pair = jnp.where(low, pair, swapped)
                q2[b] = head_rows(query)
                do2[b] = head_rows(grad)
                kk[b] = key_pair.astype(bf16)
                vv[b] = jnp.where(low, swapped, pair).astype(bf16)
                kt[b] = key_pair.T.astype(bf16)
                inner = (grad.astype(f32) * o_ref[m, pl.ds(256 * b, 256), :]).T
                delta[b, :, pl.ds(0, 256)] = jnp.sum(inner[:64], axis=0, keepdims=True)
                delta[b, :, pl.ds(256, 256)] = jnp.sum(inner[64:], axis=0, keepdims=True)
            for kb in range(4):
                grad_key = jnp.zeros((256, 128), f32)
                grad_value = jnp.zeros((256, 128), f32)
                for qb in range(kb, 4):
                    scores = dot_cols(kk[kb], q2[qb])
                    log_total = jnp.concatenate(
                        [l_ref[m, pl.ds(i, 1), pl.ds(256 * qb, 256)] for i in range(2)], 1
                    )
                    start = starts[:, 256 * qb : 256 * qb + 256]
                    s = 256 * kb + lax.broadcasted_iota(jnp.int32, (256, 512), 0)
                    keep = s >= jnp.concatenate([start, start], 1)
                    if kb == qb:
                        t = lax.broadcasted_iota(jnp.int32, (256, 512), 1)
                        keep = keep & (s <= 256 * qb + lax.rem(t, 256))
                    probs = jnp.where(keep, jnp.exp(scores - log_total), 0.0)
                    grad_probs = dot_cols(vv[kb], do2[qb])
                    grad_scores = (probs * (grad_probs - delta[qb])).astype(bf16)
                    grad_value = grad_value + dot(probs.astype(bf16), do2[qb])
                    grad_key = grad_key + dot(grad_scores, q2[qb])
                    grad_query = dot(kt[kb], grad_scores)
                    if kb == 0:
                        dq[qb] = grad_query[:64]
                    else:
                        dq[qb] = dq[qb] + grad_query[:64]
                grad_key = grad_key + pltpu.roll(grad_key, 64, 1)
                grad_value = grad_value + pltpu.roll(grad_value, 64, 1)
                tile = jnp.where(low, grad_key, grad_value).astype(bf16)
                for half in range(2):
                    rows = slice(128 * half, 128 * half + 128)
                    t_out[m, 2 * kb + half, :, pl.ds(128, 128)] = tile[rows]
            for qb in range(4):
                stacked = jnp.concatenate([dq[qb, :, pl.ds(0, 256)], dq[qb, :, pl.ds(256, 256)]], 0)
                tile = (stacked * 0.125).T.astype(bf16)
                for half in range(2):
                    rows = slice(128 * half, 128 * half + 128)
                    t_out[m, 2 * qb + half, :, pl.ds(0, 128)] = tile[rows]
            grads_back.send(m)

        heads_back(0)
        both.takes(0)
        down.takes(1)
        both.sent([0])
        for dim in range(6):
            pl.semaphore_signal(
                free_sem, inc=1, device_id=place.neighbour(dim), device_id_type=MESH
            )
        heads_back(1)

        own_loads = [
            pltpu.make_async_copy(na_hbm, own.at[0], l_sems.at[2]),
            pltpu.make_async_copy(att_hbm, own.at[1], l_sems.at[3]),
        ]
        for load in own_loads:
            load.start()
        to_na.wait_recv()
        nat[:, other_rows] = xboth[0].T
        to_att.wait_recv()
        attt[:, other_rows] = xboth[1].T
        for load in own_loads:
            load.wait()
        nat[:, own_rows] = own[0].T
        attt[:, own_rows] = own[1].T
        to_dm.wait_recv()
        cols[own_rows, pl.ds(1024, 512)] = dm_own[core]
        cols[other_rows, pl.ds(1024, 512)] = dmin[...]
        pl.semaphore_wait(free_sem, 6)

        def projection_cols(s):
            left = nat if s < 4 else attt
            for x_hi in range(2):
                part = dot(left[pl.ds(512 * x_hi, 512), :], cols[:, pl.ds(256 * s, 256)])
                reorder_store(part, g_first, s, x_hi, pl.ds(0, 256), 256)
            quad.send(s, 0)

        for s in range(4, 6):
            projection_cols(s)
        both.takes(1)
        down.takes(2)

        for load in loads[3:6]:
            load.wait()
        gain_q, gain_k = gain_tiles(qk_gain_ref[...])
        for m in range(2):
            grads_back.arrived(m)

        def both_rows(j, at):
            return jnp.concatenate([t_at(m, j)[:, pl.ds(at, 128)] for m in range(2)], 0).astype(f32)

        def head_back(grad, value, gain):
            grad = grad * cos_ref[...] + turn_heads(grad * sin_ref[...])
            scale = lax.rsqrt(head_mean(value * value) + norm_eps)
            normed = value * scale
            grad_e = grad * gain
            gain_grad = jnp.sum(grad * normed, axis=0, keepdims=True)
            return scale * (grad_e - normed * head_mean(grad_e * normed)), gain_grad

        sum_q = jnp.zeros((1, 128), f32)
        sum_k = jnp.zeros((1, 128), f32)
        for j in range(8):
            back, part = head_back(both_rows(j, 0), proj_ref[:, pl.ds(128 * j, 128)], gain_q)
            dp[0, :, pl.ds(128 * j, 128)] = back.astype(bf16)
            sum_q = sum_q + part
        for i in range(4):
            first = both_rows(2 * i, 128)
            second = both_rows(2 * i + 1, 128)
            grad_key = jnp.where(low, first, pltpu.roll(second, 64, 1))
            grad_value = jnp.where(low, pltpu.roll(first, 64, 1), second)
            back, part = head_back(grad_key, proj_ref[:, pl.ds(1024 + 128 * i, 128)], gain_k)
            dp[1, :, pl.ds(128 * i, 128)] = back.astype(bf16)
            dp[1, :, pl.ds(512 + 128 * i, 128)] = grad_value.astype(bf16)
            sum_k = sum_k + part
        to_dp = push(place, dp.at[1 - core], dpin, x_send.at[7], x_recv.at[7], partner)
        to_dp.start()
        sum_q = sum_q + pltpu.roll(sum_q, 64, 1)
        sum_k = sum_k + pltpu.roll(sum_k, 64, 1)
        vec[0, pl.ds(16, 8), :] = jnp.zeros((8, 128), f32)
        vec[0, pl.ds(16, 1), :] = jnp.where(
            lax.broadcasted_iota(jnp.int32, (1, 128), 1) < 64, sum_q, sum_k
        )
        cols[own_rows, pl.ds(0, 1024)] = dp[core]
        to_dp.wait_recv()
        cols[other_rows, pl.ds(0, 1024)] = dpin[...]
        for s in range(4):
            projection_cols(s)

        loads[6].wait()
        loads[7].wait()
        inputs = x_ref[...].astype(f32)
        scale = lax.rsqrt(jnp.mean(inputs * inputs, axis=-1, keepdims=True) + norm_eps)
        normed = inputs * scale
        grad_n = dot_cols(dp[0], w_qkv[:, pl.ds(0, 1024)]) + dot_cols(
            dp[1], w_qkv[:, pl.ds(1024, 1024)]
        )
        gain_grad = jnp.sum(grad_n * normed, axis=0, keepdims=True)
        grad_e = grad_n * gain_ref[...]
        gtok[...] = dmid[...] + scale * (
            grad_e - normed * jnp.mean(grad_e * normed, axis=-1, keepdims=True)
        )
        gtok_copy = pltpu.make_async_copy(gtok, gtok_hbm, l_sems.at[1])
        gtok_copy.start()
        for i in range(8):
            vec[0, pl.ds(i, 1), :] = gain_grad[:, 128 * i : 128 * i + 128]
        gtok_copy.wait()
        to_dp.wait_send()
        grads_back.sent()

    pl.run_scoped(
        attention_back,
        pltpu.VMEM((1024, 2048), bf16),
        pltpu.VMEM((256, 1024), bf16),
        pltpu.VMEM((256, 1024), f32),
        pltpu.VMEM((256, 128), f32),
        pltpu.VMEM((256, 128), f32),
        pltpu.VMEM((256, 1536), f32),
        pltpu.VMEM((2, 8, 128, 256), bf16),
        pltpu.VMEM((2, 1024, 128), f32),
        pltpu.VMEM((2, 2, 1024), f32),
        pltpu.VMEM((4, 512, 128), bf16),
        pltpu.VMEM((4, 512, 128), bf16),
        pltpu.VMEM((4, 256, 128), bf16),
        pltpu.VMEM((4, 256, 128), bf16),
        pltpu.VMEM((4, 128, 256), bf16),
        pltpu.VMEM((4, 1, 512), f32),
        pltpu.VMEM((4, 64, 512), f32),
        pltpu.VMEM((2, 256, 1024), bf16),
        pltpu.VMEM((2, 256, 1024), bf16),
        pltpu.VMEM((1024, 512), bf16),
        pltpu.VMEM((1024, 512), bf16),
        pltpu.VMEM((512, 1536), bf16),
        pltpu.VMEM((2, 8, 128, 256), bf16),
    )

    def vec_move(step):
        device = place.neighbour(step) if step < 6 else partner
        return push(place, vec.at[step], vec_in.at[step], v_send.at[step], v_recv.at[step], device)

    vec_move(0).start()

    def vec_take(step):
        vec_move(step).wait_recv()
        vec[step + 1] = vec[step] + vec_in[step]
        vec_move(step + 1).start()

    both.takes(2)
    down.takes(3)
    quad.takes(0)
    vec_take(0)
    both.takes(3)
    down.takes(4)
    quad.takes(1)
    vec_take(1)
    both.takes(4)
    finish_down(place, down, d_acc, d_stage, d_in, f_send, f_recv, gdn_ref)
    quad.takes(2)
    vec_take(2)
    for s in range(6):
        total = both.last(s)
        g_fin[0, s] = total[:8]
        g_fin[1, s] = total[8:]
    swap = push(place, g_fin.at[1 - core], g_in, x_send.at[8], x_recv.at[8], partner)
    swap.start()
    quad.takes(3)
    vec_take(3)
    for s in range(6):
        base = (s // 3) * 4608 + (s % 3) * 768
        ggu_ref[:, pl.ds(pl.multiple_of(base + core * FF_HALF, 256), 768)] = g_fin[core, s]
    quad.takes(4)
    vec_take(4)
    swap.wait_recv()
    for s in range(6):
        base = (s // 3) * 4608 + (s % 3) * 768
        ggu_ref[:, pl.ds(pl.multiple_of(base + (1 - core) * FF_HALF, 256), 768)] = g_in[s]
    for s in range(6):
        total = quad.last(s)
        q_fin[0, s] = total[:8]
        q_fin[1, s] = total[8:]
    swap_q = push(place, q_fin.at[1 - core], q_in, x_send.at[9], x_recv.at[9], partner)
    swap_q.start()
    vec_take(5)
    for s in range(4):
        gqkv_ref[:, pl.ds(pl.multiple_of(core * 1024 + 256 * s, 256), 256)] = q_fin[core, s]
    for s in range(4, 6):
        gout_ref[:, pl.ds(pl.multiple_of(core * 512 + 256 * (s - 4), 256), 256)] = q_fin[core, s]
    swap_q.wait_recv()
    for s in range(4):
        gqkv_ref[:, pl.ds(pl.multiple_of((1 - core) * 1024 + 256 * s, 256), 256)] = q_in[s]
    for s in range(4, 6):
        gout_ref[:, pl.ds(pl.multiple_of((1 - core) * 512 + 256 * (s - 4), 256), 256)] = q_in[s]
    vec_move(6).wait_recv()
    vec_out[...] = vec[6] + vec_in[6]

    for move in (to_dy, to_na, to_att, to_dm, swap, swap_q):
        move.wait_send()
    out_copy.wait()
    for step in range(7):
        vec_move(step).wait_send()
    down.sent()
    both.sent(range(1, 6))
    quad.sent()
    grads_out.sent()


def main_part(bounds, *arrays):
    vmem = pl.BlockSpec(memory_space=pltpu.VMEM)
    hbm = pl.BlockSpec(memory_space=pl.ANY)
    smem = pl.BlockSpec(memory_space=pltpu.SMEM)
    dma = pltpu.SemaphoreType.DMA
    return pl.pallas_call(
        main_kernel,
        out_shape=(
            jax.ShapeDtypeStruct((256, 1024), bf16),
            jax.ShapeDtypeStruct((256, 1024), f32),
            jax.ShapeDtypeStruct((8, 9216), f32),
            jax.ShapeDtypeStruct((36, 1024), f32),
            jax.ShapeDtypeStruct((8, 2048), f32),
            jax.ShapeDtypeStruct((8, 1024), f32),
            jax.ShapeDtypeStruct((24, 128), f32),
        ),
        in_specs=[smem] + [vmem] * 4 + [hbm] * 14,
        out_specs=(hbm, hbm) + (vmem,) * 5,
        scratch_shapes=[
            pltpu.VMEM((6, 64, 16, 768), bf16),
            pltpu.VMEM((6, 63, 16, 768), bf16),
            pltpu.VMEM((6, 64, 48, 128), bf16),
            pltpu.VMEM((6, 63, 48, 128), bf16),
            pltpu.VMEM((512, 1024), bf16),
            pltpu.VMEM((512, 1024), bf16),
            pltpu.VMEM((256, 1024), bf16),
            pltpu.VMEM((2, 256, 1024), bf16),
            pltpu.VMEM((2, 256, 1024), bf16),
            pltpu.VMEM((256, 1024), f32),
            pltpu.VMEM((2, 8, 128, 128), bf16),
            pltpu.VMEM((2, 8, 128, 128), bf16),
            pltpu.VMEM((256, 1024), bf16),
            pltpu.VMEM((256, 512), bf16),
            pltpu.VMEM((2, 256, 512), bf16),
            pltpu.VMEM((2, 6, 8, 768), f32),
            pltpu.VMEM((6, 8, 768), f32),
            pltpu.VMEM((144, 256), f32),
            pltpu.VMEM((4, 40, 256), f32),
            pltpu.VMEM((4, 40, 256), f32),
            pltpu.VMEM((2, 6, 8, 256), f32),
            pltpu.VMEM((6, 8, 256), f32),
            pltpu.VMEM((7, 24, 128), f32),
            pltpu.VMEM((7, 24, 128), f32),
            dma((9,)),
            dma((5,)),
            dma((10,)),
            dma((10,)),
            dma((6, 6)),
            dma((6, 6)),
            dma((6, 6)),
            dma((6, 6)),
            dma((6, 6)),
            dma((6, 6)),
            dma((4,)),
            dma((4,)),
            dma((2, 7)),
            dma((2, 7)),
            dma((2, 7)),
            dma((2, 7)),
            dma((7,)),
            dma((7,)),
            pltpu.SemaphoreType.REGULAR,
        ],
        compiler_params=pltpu.CompilerParams(
            collective_id=0, has_side_effects=True, vmem_limit_bytes=VMEM_LIMIT
        ),
        name="feed_forward_and_backward",
    )(bounds, *arrays)


def tables(positions):
    lane = jnp.arange(128, dtype=jnp.int32)
    freqs = rope_theta ** (-2.0 * (lane % 32).astype(f32) / 64)
    angles = positions.astype(f32)[:, None] * freqs[None, :]
    return jnp.cos(angles), jnp.sin(angles) * jnp.where(lane % 64 < 32, -1.0, 1.0)


def local(
    tokens,
    cotangent,
    bounds,
    positions,
    norm_gain_attn,
    w_qkv,
    qk_gain,
    w_out,
    norm_gain_ffn,
    w_gate_up,
    w_down,
):
    x = tokens.reshape(256, 1024)
    cot = cotangent.reshape(256, 1024)
    cosine, sine = tables(positions.reshape(256))
    mid, na, att, proj, qkv, o, l = attention(
        bounds, x, cosine, sine, norm_gain_attn[None], qk_gain[None], w_qkv, w_out
    )
    layer_out, grad_tokens, sum_gate_up, sum_down, sum_qkv, sum_out, vec = main_part(
        bounds,
        mid,
        norm_gain_ffn[None],
        norm_gain_attn[None],
        qk_gain[None],
        cot,
        x,
        cosine,
        sine,
        na,
        att,
        proj,
        qkv,
        o,
        l,
        w_gate_up,
        w_down,
        w_qkv,
        w_out,
    )
    own = lax.axis_index("rows") * 8 + lax.axis_index("ctx")
    return (
        layer_out.reshape(tokens.shape),
        grad_tokens.reshape(tokens.shape),
        lax.dynamic_slice(vec[:8].reshape(1024), (own * 8,), (8,)),
        sum_qkv,
        lax.dynamic_slice(vec[16], (own,), (1,)),
        sum_out,
        lax.dynamic_slice(vec[8:16].reshape(1024), (own * 8,), (8,)),
        sum_gate_up,
        sum_down,
    )


def solution(mesh):
    placed = (
        P(None, "rows", "ctx", None),
        P(None, "rows", "ctx", None),
        P(None, "rows", None),
        P(None, "rows", "ctx"),
        P(),
        P(),
        P(),
        P(),
        P(),
        P(),
        P(),
    )
    return jax.shard_map(
        local,
        mesh=mesh,
        in_specs=placed,
        out_specs=(
            P(None, "rows", "ctx", None),
            P(None, "rows", "ctx", None),
            P(("rows", "ctx")),
            P(("rows", "ctx"), None),
            P(("rows", "ctx")),
            P(("rows", "ctx"), None),
            P(("rows", "ctx")),
            P(("rows", "ctx"), None),
            P(("rows", "ctx"), None),
        ),
        check_vma=False,
    )
```

time: 206 us -> 186 us (0.903)
  Pallas kernels: 191 us -> 169 us
    pallas_call x2 -> x1, Pallas kernels: 158 us -> 137 us  [main_part(): pl.pallas_call(main_kernel, out_shape=(jax.ShapeDtypeStruct((256, 1024),...]
    unnamed x8 -> x6, local copies, waits for them, and re-layouts: 9.38 us -> 10.3 us
where the time goes in v3:
time: 186 us; the launch traced here: 185 us
  Pallas kernels  169 us (91%)
  local copies, waits for them, and re-layouts  13.4 us (7%)
  other arithmetic  1.93 us (1%)
    pallas_call x1, Pallas kernels, main_part(): pl.pallas_call(main_kernel, out_shape=(jax.ShapeDtypeStruct((256, 1024),...  137 us
    pallas_call x1, Pallas kernels, attention(): pl.pallas_call(attention_kernel, out_shape=(jax.ShapeDtypeStruct((256, 10...  32.7 us
    unnamed x6, local copies, waits for them, and re-layouts  10.3 us

profile of v3, /device:TPU:1, one launch (start us, length us, event | category | flops | bytes accessed | tf_op | source)
XLA Modules:
  0.0 185.3 jit_solution(94821277329731394)
XLA Ops:
  0.7 0.7 convert_element_type.17
  1.3 1.2 fusion
  2.6 32.7 %attention_forward.1 = (f32[256,1024]{1,0:T(8,128)}, bf16[256,1024]{1,0:T(8,128)(2,1)}, bf16[256,1024]{1,0:T(8,128)(2,1)}, f32[256,1536]{1,0:T(8,128)}, bf16[2,8...) custom-call(s32[2,1,5]{2,1,0:T(1,128)} %bounds_ref.3, bf16[256,1024]{1,0:T(8,128)(2,1)} %bitcast.17, ...), custom_call_target="tpu_custom_call" | custom-call | tf_op jit(solution)/shard_map/attention_forward/pallas_call | solution.py:444
  35.3 136.5 %feed_forward_and_backward.1 = (bf16[256,1024]{1,0:T(8,128)(2,1)}, f32[256,1024]{1,0:T(8,128)}, f32[8,9216]{1,0:T(8,128)}, f32[36,1024]{1,0:T(8,128)}, f32[8,204...) custom-call(s32[2,1,5]{2,1,0:T(1,128)} %bounds_ref.3, f32[256,1024]{1,0:T(8,128)} %get-tuple-element.23.mid_ref, ...), custom_call_target="tpu_custom_call" | custom-call | tf_op jit(solution)/shard_map/feed_forward_and_backward/pallas_call | solution.py:1048
  171.8 0.7 slice_bitcast_fusion
  172.5 0.6 dynamic_slice.11
  173.1 0.6 dynamic_slice.14
  173.7 0.7 slice.10
  174.4 0.6 constant_dynamic-slice_fusion
  174.9 1.9 %copy.28 = bf16[2,1,128,1024]{3,2,1,0:T(8,128)(2,1)} copy(bf16[2,1,128,1024]{3,2,1,0:T(8,128)(2,1)} %bitcast.21) | data formatting | bytes 1048576
  176.8 2.3 %copy.29 = f32[2,1,128,1024]{3,2,1,0:T(8,128)} copy(f32[2,1,128,1024]{3,2,1,0:T(8,128)} %bitcast.19) | data formatting | bytes 2097152
  179.1 1.5 copy.30
  180.6 1.4 copy.31
  182.0 1.7 copy.32
  183.7 1.6 copy.33
  (1 shorter events, 0.0 us)
